TPU v7x, 512 devices: a whole 4x4x16 slice. The times are simulated.
512 devices in a mesh: dp: 8 (over x, z_hi), dap: 64 (over z_lo, y, core).
Axes of the slice: x: 4, y: 4, z: 16 (z_hi: 2, z_lo: 8; z = z_hi * 8 + z_lo), core: 2. Of those that a mesh axis runs over, the one named last changes fastest.
Arguments:
- alignment: bfloat16 [2048, 512, 256], P(('dp', 'dap')), parts along dimension 0, may hold values from -6 to 6
- pair_act: bfloat16 [4096, 512, 128], P(('dp', 'dap')), parts along dimension 0, may hold values from -6 to 6
- crop_mask: int32 [4096], P('dp'), parts along dimension 0, may hold values 0 or 1
- seq_mask: int32 [2048], P('dp'), parts along dimension 0, may hold values 0 or 1
- chain_ids: int32 [4096], P('dp'), parts along dimension 0, may hold values from 0 to 3, never falling along the last dimension, each value on 1 to 256 neighbouring positions
- chain_embed: float32 [2, 128], replicated, may hold values from -6 to 6
- score_proj: bfloat16 [2, 256, 256], replicated, may hold values from -40 to 40
- value_gate: bfloat16 [2, 256, 256], replicated, may hold values from -0.375 to 0.375
- column_out: bfloat16 [256, 256], replicated, may hold values from -0.375 to 0.375
- triangle_in: bfloat16 [2, 128, 640], replicated, may hold values from -0.5 to 0.5
- triangle_out: bfloat16 [2, 128, 128], replicated, may hold values from -0.5 to 0.5
Outputs:
- alignment_new: bfloat16 [2048, 512, 256], P('dp', 'dap'), parts along dimension 0
- pair_new: bfloat16 [4096, 512, 128], P(('dp', 'dap')), parts along dimension 0
There are 8 independent parts, one for each index of `dp`. A program takes and returns all parts, laid end to end along the dimension named above; an argument that names none is the same for every part. Nothing has to cross between parts.
All inputs are finite; a program needn't handle non-finite values.
Results may differ from a plain program's by a relative error of at most 0.004.
The roundings to bfloat16 on the way count: a program that leaves them out, or rounds other values in their place, can miss the bound.
Values may be sent and summed in bfloat16 or wider, within the bound.
No kernel may reach another device: no remote copies, remote signals or barrier semaphores. Data moves between devices by JAX's collectives and lax.ppermute only.
A program may use at most 64 MiB of HBM per device.

v0:
```python
import jax
import jax.numpy as jnp
from jax import lax
from jax.sharding import PartitionSpec as P

HEADS = 8
HEAD_DIM = 32


EPS = 1e-05


def normalize(values, axis):
    average = jnp.mean(values, axis=axis, keepdims=True)
    centered = values - average
    variance = jnp.mean(centered * centered, axis=axis, keepdims=True)
    return centered * lax.rsqrt(variance + EPS)


def column_update(column, key_bias, score_proj, value_gate, column_out):
    count = column.shape[0]
    normed = normalize(column.astype(jnp.float32), 1).astype(jnp.bfloat16)
    queries = (
        jnp.dot(normed, score_proj[0], preferred_element_type=jnp.float32) * HEAD_DIM ** (-0.5)
    ).astype(jnp.bfloat16)
    key_rows = jnp.dot(normed, score_proj[1], preferred_element_type=jnp.float32).astype(
        jnp.bfloat16
    )
    value_rows = jnp.dot(normed, value_gate[0], preferred_element_type=jnp.float32).astype(
        jnp.bfloat16
    )
    gate_rows = jax.nn.sigmoid(jnp.dot(normed, value_gate[1], preferred_element_type=jnp.float32))
    queries = queries.reshape(count, HEADS, HEAD_DIM)
    key_rows = key_rows.reshape(count, HEADS, HEAD_DIM)
    value_rows = value_rows.reshape(count, HEADS, HEAD_DIM)
    scores = (
        jnp.einsum("shd,thd->hst", queries, key_rows, preferred_element_type=jnp.float32)
        + key_bias[None, None, :]
    )
    highest = jnp.max(scores, axis=-1, keepdims=True)
    raised = jnp.exp(scores - highest)
    weights = (raised / jnp.sum(raised, axis=-1, keepdims=True)).astype(jnp.bfloat16)
    mixture = jnp.einsum(
        "hst,thd->shd", weights, value_rows, preferred_element_type=jnp.float32
    ).reshape(count, HEADS * HEAD_DIM)
    gated = (gate_rows * mixture).astype(jnp.bfloat16)
    return (
        column.astype(jnp.float32) + jnp.dot(gated, column_out, preferred_element_type=jnp.float32)
    ).astype(jnp.bfloat16)


def project_pair(pair_sum, pair_mask, weights_in, width):
    normed = normalize(pair_sum, 2).astype(jnp.bfloat16)
    projected = jnp.einsum(
        "ijd,de->iej", normed, weights_in[:, : 4 * width], preferred_element_type=jnp.float32
    )
    left_part = (
        jax.nn.sigmoid(projected[:, :width])
        * projected[:, width : 2 * width]
        * pair_mask[:, None, :]
    ).astype(jnp.bfloat16)
    right_part = (
        jax.nn.sigmoid(projected[:, 2 * width : 3 * width])
        * projected[:, 3 * width : 4 * width]
        * pair_mask[:, None, :]
    ).astype(jnp.bfloat16)
    gate_part = jax.nn.sigmoid(
        jnp.einsum(
            "ijd,de->ije", normed, weights_in[:, 4 * width :], preferred_element_type=jnp.float32
        )
    )
    return (left_part, right_part, gate_part)


def return_products(products):
    return lax.all_to_all(products, "dap", split_axis=0, concat_axis=1, tiled=True)


def finish_triangle(pair_sum, products, gate_part, weights_out):
    normed_products = normalize(products.astype(jnp.float32), 1).astype(jnp.bfloat16)
    update = jnp.einsum(
        "icj,cd->ijd", normed_products, weights_out, preferred_element_type=jnp.float32
    )
    return pair_sum + gate_part * update


def on_device(
    alignment,
    pair_act,
    crop_mask,
    seq_mask,
    chain_ids,
    chain_embed,
    score_proj,
    value_gate,
    column_out,
    triangle_in,
    triangle_out,
):
    rows_here = pair_act.shape[0]
    width = triangle_out.shape[1]
    devices = lax.axis_size("dap")
    row_start = lax.axis_index("dap") * rows_here
    kept_rows = jnp.maximum(seq_mask, (jnp.arange(seq_mask.shape[0]) == 0).astype(jnp.int32))
    key_bias = (kept_rows - 1).astype(jnp.float32) * 1000000000.0
    crop = crop_mask.astype(jnp.float32)
    crop_rows = lax.dynamic_slice_in_dim(crop, row_start, rows_here)
    pair_mask = crop_rows[:, None] * crop[None, :]
    chain_rows = lax.dynamic_slice_in_dim(chain_ids, row_start, rows_here)
    same_chain = chain_rows[:, None] == chain_ids[None, :]
    pair_sum = pair_act.astype(jnp.float32) + jnp.where(
        same_chain[:, :, None], chain_embed[0], chain_embed[1]
    )
    left_part, right_part, gate_part = project_pair(pair_sum, pair_mask, triangle_in[0], width)
    seq_here = alignment.shape[0]
    blocked = alignment.reshape(seq_here, devices, rows_here, alignment.shape[2])
    attend_blocked = lax.all_to_all(blocked, "dap", split_axis=1, concat_axis=0, tiled=True)
    by_column = jnp.moveaxis(attend_blocked[:, 0], 1, 0)
    attended = lax.map(
        lambda column: column_update(column, key_bias, score_proj, value_gate, column_out),
        by_column,
    )
    attended = jnp.moveaxis(attended, 0, 1)[:, None]
    alignment_new = attended.reshape(attended.shape[0], rows_here, alignment.shape[2])
    left_all, right_all = (
        lax.all_to_all(left_part, "dap", split_axis=1, concat_axis=0, tiled=True),
        lax.all_to_all(right_part, "dap", split_axis=1, concat_axis=0, tiled=True),
    )
    products = jnp.einsum(
        "ick,jck->icj", left_all, right_all, preferred_element_type=jnp.float32
    ).astype(jnp.bfloat16)
    pair_sum = finish_triangle(pair_sum, return_products(products), gate_part, triangle_out[0])
    left_part, right_part, gate_part = project_pair(pair_sum, pair_mask, triangle_in[1], width)
    left_all, right_all = (
        lax.all_to_all(left_part, "dap", split_axis=1, concat_axis=0, tiled=True),
        lax.all_to_all(right_part, "dap", split_axis=1, concat_axis=0, tiled=True),
    )
    products = jnp.einsum(
        "kci,kcj->icj", left_all, right_all, preferred_element_type=jnp.float32
    ).astype(jnp.bfloat16)
    pair_sum = finish_triangle(pair_sum, return_products(products), gate_part, triangle_out[1])
    return (alignment_new, pair_sum.astype(jnp.bfloat16))


def solution(mesh):
    placed = (
        P(("dp", "dap"), None, None),
        P(("dp", "dap"), None, None),
        P("dp"),
        P("dp"),
        P("dp"),
        P(),
        P(),
        P(),
        P(),
        P(),
        P(),
    )
    return jax.shard_map(
        on_device,
        mesh=mesh,
        in_specs=placed,
        out_specs=(P("dp", "dap", None), P(("dp", "dap"), None, None)),
        check_vma=False,
    )
```

profile of v0, /device:TPU:1, one launch (start us, length us, event | category | flops | bytes accessed | tf_op | source)
XLA Modules:
  0.0 506.6 jit_solution(4292721204272594633)
XLA Ops:
  8.4 1.7 copy.167
  10.1 17.4 %all-to-all-start.1 = ((bf16[8,128,512]{2,0,1:T(8,128)(2,1)}), bf16[8,128,512]{2,0,1:T(8,128)(2,1)}, u32[]{:S(2)}, u32[]{:S(2)}) async-start(bf16[8,128,512]{2,0,1:T(8,128)(2,1)} %copy.167), calls=%async_computation.1 | async-start | bytes 2097152 | tf_op jit(solution)/shard_map/all_to_all | solution.py:127
  28.4 50.5 %all-to-all-done.1 = bf16[8,128,512]{2,0,1:T(8,128)(2,1)} async-done(((bf16[8,128,512]{2,0,1:T(8,128)(2,1)}), bf16[8,128,512]{2,0,1:T(8,128)(2,1)}, u32[]{:S(2)}, u32[]{:S(2)}) %all-to-all-start.1) | async-done | bytes 1048608 | tf_op jit(solution)/shard_map/all_to_all | solution.py:127
  78.9 59.1 %all_to_all.105 = bf16[8,128,512]{2,0,1:T(8,128)(2,1)S(1)} all-to-all(bf16[8,128,512]{2,0,1:T(8,128)(2,1)S(1)} %copy.169), channel_id=1, replica_groups=mesh['dp'=8,'dap'=64] {'dap'}, dimensions={1} | all-to-all | bytes 2097152 | tf_op jit(solution)/shard_map/all_to_all | solution.py:126
  137.9 2.9 fusion.77
  140.9 3.7 copy.171
  144.6 7.8 %all-to-all-start.3 = ((bf16[512,2,512]{2,1,0:T(2,128)(2,1)}), bf16[512,2,512]{2,1,0:T(2,128)(2,1)S(1)}, u32[]{:S(2)}, u32[]{:S(2)}) async-start(bf16[512,2,512]{2,1,0:T(2,128)(2,1)} %copy.171), calls=%async_computation.3 | async-start | bytes 2097152 | tf_op jit(solution)/shard_map/all_to_all | solution.py:76
  152.5 1.8 copy.158
  154.3 49.7 %all-to-all-done.3 = bf16[512,2,512]{2,1,0:T(2,128)(2,1)S(1)} async-done(((bf16[512,2,512]{2,1,0:T(2,128)(2,1)}), bf16[512,2,512]{2,1,0:T(2,128)(2,1)S(1)}, u32[]{:S(2)}, u32[]{:S(2)}) %all-to-all-start.3) | async-done | bytes 1048608 | tf_op jit(solution)/shard_map/all_to_all | solution.py:76
  203.9 8.0 %all-to-all-start = ((bf16[4,64,8,256]{3,0,2,1:T(4,128)(2,1)}), bf16[4,64,8,256]{3,0,2,1:T(4,128)(2,1)}, u32[]{:S(2)}, u32[]{:S(2)}) async-start(bf16[4,64,8,256]{3,0,2,1:T(4,128)(2,1)} %bitcast.12), calls=%async_computation | async-start | bytes 2097152 | tf_op jit(solution)/shard_map/all_to_all | solution.py:117
  217.1 2.0 fusion.49
  219.1 2.7 copy.179
  221.8 41.6 %all-to-all-done = bf16[4,64,8,256]{3,0,2,1:T(4,128)(2,1)} async-done(((bf16[4,64,8,256]{3,0,2,1:T(4,128)(2,1)}), bf16[4,64,8,256]{3,0,2,1:T(4,128)(2,1)}, u32[]{:S(2)}, u32[]{:S(2)}) %all-to-all-start) | async-done | bytes 1048608 | tf_op jit(solution)/shard_map/all_to_all | solution.py:117
  263.3 8.0 %all-to-all-start.4 = ((bf16[8,128,512]{2,0,1:T(8,128)(2,1)}), bf16[8,128,512]{2,0,1:T(8,128)(2,1)}, u32[]{:S(2)}, u32[]{:S(2)}) async-start(bf16[8,128,512]{2,0,1:T(8,128)(2,1)} %copy.179), calls=%async_computation.4 | async-start | bytes 2097152 | tf_op jit(solution)/shard_map/all_to_all | solution.py:136
  271.4 1.7 copy.181
  273.1 49.6 %all-to-all-done.4 = bf16[8,128,512]{2,0,1:T(8,128)(2,1)} async-done(((bf16[8,128,512]{2,0,1:T(8,128)(2,1)}), bf16[8,128,512]{2,0,1:T(8,128)(2,1)}, u32[]{:S(2)}, u32[]{:S(2)}) %all-to-all-start.4) | async-done | bytes 1048608 | tf_op jit(solution)/shard_map/all_to_all | solution.py:136
  322.7 7.8 %all-to-all-start.5 = ((bf16[8,128,512]{2,0,1:T(8,128)(2,1)}), bf16[8,128,512]{2,0,1:T(8,128)(2,1)S(1)}, u32[]{:S(2)}, u32[]{:S(2)}) async-start(bf16[8,128,512]{2,0,1:T(8,128)(2,1)} %copy.181), calls=%async_computation.5 | async-start | bytes 2097152 | tf_op jit(solution)/shard_map/all_to_all | solution.py:135
  333.2 48.8 %all-to-all-done.5 = bf16[8,128,512]{2,0,1:T(8,128)(2,1)S(1)} async-done(((bf16[8,128,512]{2,0,1:T(8,128)(2,1)}), bf16[8,128,512]{2,0,1:T(8,128)(2,1)S(1)}, u32[]{:S(2)}, u32[]{:S(2)}) %all-to-all-start.5) | async-done | bytes 1048608 | tf_op jit(solution)/shard_map/all_to_all | solution.py:135
  382.0 3.0 fusion.78
  385.0 3.7 copy.184
  388.7 7.8 %all-to-all-start.6 = ((bf16[512,2,512]{2,1,0:T(2,128)(2,1)}), bf16[512,2,512]{2,1,0:T(2,128)(2,1)S(1)}, u32[]{:S(2)}, u32[]{:S(2)}) async-start(bf16[512,2,512]{2,1,0:T(2,128)(2,1)} %copy.184), calls=%async_computation.6 | async-start | bytes 2097152 | tf_op jit(solution)/shard_map/all_to_all | solution.py:76
  396.6 100.2 %while.10 = (s32[]{:T(128)}, bf16[8,256,256]{2,1,0:T(8,128)(2,1)}, bf16[8,256,256]{2,1,0:T(8,128)(2,1)}, bf16[2,256,256]{2,1,0:T(8,128)(2,1)}, bf16[2,256,256]{2...) while((s32[]{:T(128)}, bf16[8,256,256]{2,1,0:T(8,128)(2,1)}, ...), condition=%wide.region_5.6_spmd, body=%wide.region_0.5_spmd.sunk | while | flops 274336512 | bytes 4886165 | solution.py:119
  402.1 1.9 convolution_convert_fusion.6
  404.1 2.0 fusion.145
  406.9 2.2 fusion.146
  414.7 1.9 convolution_convert_fusion.6
  416.6 2.0 fusion.145
  419.4 2.2 fusion.146
  427.2 1.9 convolution_convert_fusion.6
  429.1 2.0 fusion.145
  431.9 2.2 fusion.146
  439.7 1.9 convolution_convert_fusion.6
  441.6 2.0 fusion.145
  444.5 2.2 fusion.146
  452.2 1.9 convolution_convert_fusion.6
  454.2 2.0 fusion.145
  457.0 2.2 fusion.146
  464.8 1.9 convolution_convert_fusion.6
  466.7 2.0 fusion.145
  469.5 2.2 fusion.146
  477.3 1.9 convolution_convert_fusion.6
  479.2 2.0 fusion.145
  482.0 2.2 fusion.146
  489.8 1.9 convolution_convert_fusion.6
  491.7 2.0 fusion.145
  494.5 2.2 fusion.146
  496.8 2.8 copy.231
  499.6 2.7 fusion.89
  (153 shorter events, 71.3 us)
Async XLA Ops:
  2.9 2.5 copy-start.3
  4.4 1.2 copy-start.4
  5.4 210.3 %copy-start.2 = (bf16[128,640]{1,0:T(8,128)(2,1)}, bf16[128,640]{1,0:T(8,128)(2,1)S(1)}, u32[]{:S(2)}) copy-start(bf16[128,640]{1,0:T(8,128)(2,1)S(1)} %get-tuple-element.77) | copy-start | bytes 491524
  10.1 68.8 %all-to-all-start.1 = ((bf16[8,128,512]{2,0,1:T(8,128)(2,1)}), bf16[8,128,512]{2,0,1:T(8,128)(2,1)}, u32[]{:S(2)}, u32[]{:S(2)}) async-start(bf16[8,128,512]{2,0,1:T(8,128)(2,1)} %copy.167), calls=%async_computation.1 | async-start | bytes 2097152 | tf_op jit(solution)/shard_map/all_to_all | solution.py:127
  140.9 11.6 %copy-start.1 = (bf16[4,512,256]{2,1,0:T(8,128)(2,1)S(1)}, bf16[4,512,256]{2,1,0:T(8,128)(2,1)}, u32[]{:S(2)}) copy-start(bf16[4,512,256]{2,1,0:T(8,128)(2,1)} %param.13) | copy-start | bytes 3145732
  144.6 59.3 %all-to-all-start.3 = ((bf16[512,2,512]{2,1,0:T(2,128)(2,1)}), bf16[512,2,512]{2,1,0:T(2,128)(2,1)S(1)}, u32[]{:S(2)}, u32[]{:S(2)}) async-start(bf16[512,2,512]{2,1,0:T(2,128)(2,1)} %copy.171), calls=%async_computation.3 | async-start | bytes 2097152 | tf_op jit(solution)/shard_map/all_to_all | solution.py:76
  203.9 59.4 %all-to-all-start = ((bf16[4,64,8,256]{3,0,2,1:T(4,128)(2,1)}), bf16[4,64,8,256]{3,0,2,1:T(4,128)(2,1)}, u32[]{:S(2)}, u32[]{:S(2)}) async-start(bf16[4,64,8,256]{3,0,2,1:T(4,128)(2,1)} %bitcast.12), calls=%async_computation | async-start | bytes 2097152 | tf_op jit(solution)/shard_map/all_to_all | solution.py:117
  213.1 0.8 copy-start.6
  263.3 59.4 %all-to-all-start.4 = ((bf16[8,128,512]{2,0,1:T(8,128)(2,1)}), bf16[8,128,512]{2,0,1:T(8,128)(2,1)}, u32[]{:S(2)}, u32[]{:S(2)}) async-start(bf16[8,128,512]{2,0,1:T(8,128)(2,1)} %copy.179), calls=%async_computation.4 | async-start | bytes 2097152 | tf_op jit(solution)/shard_map/all_to_all | solution.py:136
  271.3 59.2 %copy-start.5 = (s32[256]{0:T(256)S(1)}, s32[256]{0:T(256)}, u32[]{:S(2)}) copy-start(s32[256]{0:T(256)} %param.16) | copy-start | bytes 3076
  322.7 59.3 %all-to-all-start.5 = ((bf16[8,128,512]{2,0,1:T(8,128)(2,1)}), bf16[8,128,512]{2,0,1:T(8,128)(2,1)S(1)}, u32[]{:S(2)}, u32[]{:S(2)}) async-start(bf16[8,128,512]{2,0,1:T(8,128)(2,1)} %copy.181), calls=%async_computation.5 | async-start | bytes 2097152 | tf_op jit(solution)/shard_map/all_to_all | solution.py:135
  388.7 113.5 %all-to-all-start.6 = ((bf16[512,2,512]{2,1,0:T(2,128)(2,1)}), bf16[512,2,512]{2,1,0:T(2,128)(2,1)S(1)}, u32[]{:S(2)}, u32[]{:S(2)}) async-start(bf16[512,2,512]{2,1,0:T(2,128)(2,1)} %copy.184), calls=%async_computation.6 | async-start | bytes 2097152 | tf_op jit(solution)/shard_map/all_to_all | solution.py:76
  400.0 4.1 copy-start.8
  401.3 2.7 copy-start.9
  412.5 4.1 copy-start.8
  413.9 2.7 copy-start.9
  425.1 4.1 copy-start.8
  426.4 2.7 copy-start.9
  437.6 4.1 copy-start.8
  438.9 2.7 copy-start.9
  450.1 4.1 copy-start.8
  451.5 2.7 copy-start.9
  462.6 4.1 copy-start.8
  464.0 2.7 copy-start.9
  475.2 4.1 copy-start.8
  476.5 2.7 copy-start.9
  487.7 4.1 copy-start.8
  489.0 2.7 copy-start.9
  502.7 1.6 copy-start
  502.7 1.6 copy-start.7
where the time goes:
time: 509 us; the launch traced here: 507 us
  waiting for transfers between devices  240 us (47%)
  matrix products  90.6 us (18%)
  blocking collectives  59.1 us (12%)
  starting transfers between devices  56.9 us (11%)
  local copies, waits for them, and re-layouts  34.8 us (7%)
  other arithmetic  23.7 us (5%)
    all_to_all x2, waiting for transfers between devices, on_device(): lax.all_to_all(right_part, 'dap', split_axis=1, concat_axis=0, tiled=True)  100 us
    all_to_all x1, blocking collectives, on_device(): lax.all_to_all(left_part, 'dap', split_axis=1, concat_axis=0, tiled=True)  59.1 us
    all_to_all x2, waiting for transfers between devices, return_products(): lax.all_to_all(products, 'dap', split_axis=0, concat_axis=1, tiled=True)  49.7 us
    all_to_all x1, waiting for transfers between devices, on_device(): lax.all_to_all(left_part, 'dap', split_axis=1, concat_axis=0, tiled=True)  48.8 us
    all_to_all x1, waiting for transfers between devices, on_device(): lax.all_to_all(blocked, 'dap', split_axis=1, concat_axis=0, tiled=True)  41.6 us
    all_to_all x2, starting transfers between devices, on_device(): lax.all_to_all(right_part, 'dap', split_axis=1, concat_axis=0, tiled=True)  25.4 us
    dot_general x8, matrix products, column_update(): jnp.dot(gated, column_out, preferred_element_type=jnp.float32)  17.8 us
    dot_general x8, matrix products, column_update(): jnp.einsum('hst,thd->shd', weights, value_rows, preferred_element_type=jn...  15.8 us
  transfers between devices with their start and end apart: 6, of which 5 were waited for; matrix products, arithmetic and copies ran while one was open for 24% of the time, Pallas kernels for 0%

commit v1 on v0

--- a/solution.py
+++ b/solution.py
@@ -1,3 +1,5 @@
+import functools
+
 import jax
 import jax.numpy as jnp
 from jax import lax
@@ -72,6 +74,18 @@
     return (left_part, right_part, gate_part)
 
 
+def exchange_parts(left_part, right_part):
+    rows, width, side = left_part.shape
+    devices = lax.axis_size("dap")
+    share = width // devices
+    both = jnp.concatenate(
+        [part.reshape(rows, devices, share, side) for part in (left_part, right_part)], axis=2
+    )
+    both = lax.all_to_all(both, "dap", split_axis=1, concat_axis=0, tiled=True)
+    both = both.reshape(rows * devices, 2 * share, side)
+    return both
+
+
 def return_products(products):
     return lax.all_to_all(products, "dap", split_axis=0, concat_axis=1, tiled=True)
 
@@ -111,33 +125,39 @@
     pair_sum = pair_act.astype(jnp.float32) + jnp.where(
         same_chain[:, :, None], chain_embed[0], chain_embed[1]
     )
-    left_part, right_part, gate_part = project_pair(pair_sum, pair_mask, triangle_in[0], width)
     seq_here = alignment.shape[0]
     blocked = alignment.reshape(seq_here, devices, rows_here, alignment.shape[2])
-    attend_blocked = lax.all_to_all(blocked, "dap", split_axis=1, concat_axis=0, tiled=True)
-    by_column = jnp.moveaxis(attend_blocked[:, 0], 1, 0)
-    attended = lax.map(
+    blocked = lax.all_to_all(blocked, "dap", split_axis=1, concat_axis=0, tiled=True)
+    by_column = jnp.moveaxis(blocked[:, 0], 1, 0)
+    attend = functools.partial(
+        lax.map,
         lambda column: column_update(column, key_bias, score_proj, value_gate, column_out),
-        by_column,
     )
-    attended = jnp.moveaxis(attended, 0, 1)[:, None]
-    alignment_new = attended.reshape(attended.shape[0], rows_here, alignment.shape[2])
-    left_all, right_all = (
-        lax.all_to_all(left_part, "dap", split_axis=1, concat_axis=0, tiled=True),
-        lax.all_to_all(right_part, "dap", split_axis=1, concat_axis=0, tiled=True),
+    left_part, right_part, gate_part = project_pair(pair_sum, pair_mask, triangle_in[0], width)
+    left_part, right_part, by_column = lax.optimization_barrier(
+        (left_part, right_part, by_column)
     )
+    both = exchange_parts(left_part, right_part)
+    half = rows_here // 2
+    first = attend(by_column[:half])
+    both, first = lax.optimization_barrier((both, first))
+    share = width // devices
     products = jnp.einsum(
-        "ick,jck->icj", left_all, right_all, preferred_element_type=jnp.float32
+        "ick,jck->icj", both[:, :share], both[:, share:], preferred_element_type=jnp.float32
     ).astype(jnp.bfloat16)
     pair_sum = finish_triangle(pair_sum, return_products(products), gate_part, triangle_out[0])
     left_part, right_part, gate_part = project_pair(pair_sum, pair_mask, triangle_in[1], width)
-    left_all, right_all = (
-        lax.all_to_all(left_part, "dap", split_axis=1, concat_axis=0, tiled=True),
-        lax.all_to_all(right_part, "dap", split_axis=1, concat_axis=0, tiled=True),
+    left_part, right_part, by_column = lax.optimization_barrier(
+        (left_part, right_part, by_column)
     )
+    both = exchange_parts(left_part, right_part)
+    second = attend(by_column[half:])
+    both, second = lax.optimization_barrier((both, second))
     products = jnp.einsum(
-        "kci,kcj->icj", left_all, right_all, preferred_element_type=jnp.float32
+        "kci,kcj->icj", both[:, :share], both[:, share:], preferred_element_type=jnp.float32
     ).astype(jnp.bfloat16)
+    attended = jnp.moveaxis(jnp.concatenate([first, second]), 0, 1)
+    alignment_new = attended.reshape(attended.shape[0], rows_here, alignment.shape[2])
     pair_sum = finish_triangle(pair_sum, return_products(products), gate_part, triangle_out[1])
     return (alignment_new, pair_sum.astype(jnp.bfloat16))
 

time: 509 us -> 438 us (0.86)
  blocking collectives: 59.1 us -> 0 us
  waiting for transfers between devices: 240 us -> 228 us
  matrix products: 90.6 us -> 97.6 us
  starting transfers between devices: 56.9 us -> 51.1 us
    all_to_all x3 -> x2, waiting for transfers between devices: 149 us -> 86.6 us  [exchange_parts(): both = lax.all_to_all(both, 'dap', split_axis=1, concat_axis=0, tiled=True)]
    all_to_all x1 -> x0, blocking collectives: 59.1 us -> none  [on_device(): lax.all_to_all(left_part, 'dap', split_axis=1, concat_axis=0, tiled=True)]
    all_to_all x2, waiting for transfers between devices: 49.7 us -> 94.8 us  [return_products(): lax.all_to_all(products, 'dap', split_axis=0, concat_axis=1, tiled=True)]
    all_to_all x3 -> x2, starting transfers between devices: 33.2 us -> 16.1 us  [exchange_parts(): both = lax.all_to_all(both, 'dap', split_axis=1, concat_axis=0, tiled=True)]
    convert_element_type x6 -> x2, local copies, waits for them, and re-layouts: 14.4 us -> 4.19 us  [the longest x1 2.1 us: on_device(): products = jnp.einsum('ick,jck->icj', both[:, :share], both[:, share:], p...]
    optimization_barrier x0 -> x6, local copies, waits for them, and re-layouts: none -> 9.6 us  [the longest x4 7.75 us: on_device(): lax.optimization_barrier((left_part, right_part, by_column))]
    all_to_all x1, starting transfers between devices: 8.03 us -> 17.5 us  [on_device(): lax.all_to_all(blocked, 'dap', split_axis=1, concat_axis=0, tiled=True)]
    sub x8, matrix products: 6.15 us -> 13.7 us  [column_update(): raised = jnp.exp(scores - highest)]
  transfers between devices with their start and end apart: 6 -> 5, of which waited for: 5 -> 5; matrix products, arithmetic and copies ran while one was open for 24% -> 27% of each run, Pallas kernels for 0% -> 0%
where the time goes in v1:
time: 438 us; the launch traced here: 436 us
  waiting for transfers between devices  228 us (52%)
  matrix products  97.6 us (22%)
  starting transfers between devices  51.1 us (12%)
  local copies, waits for them, and re-layouts  35.5 us (8%)
  other arithmetic  23.1 us (5%)
    all_to_all x2, waiting for transfers between devices, return_products(): lax.all_to_all(products, 'dap', split_axis=0, concat_axis=1, tiled=True)  94.8 us
    all_to_all x2, waiting for transfers between devices, exchange_parts(): both = lax.all_to_all(both, 'dap', split_axis=1, concat_axis=0, tiled=True)  86.6 us
    all_to_all x1, waiting for transfers between devices, on_device(): lax.all_to_all(blocked, 'dap', split_axis=1, concat_axis=0, tiled=True)  46.2 us
    all_to_all x1, starting transfers between devices, on_device(): lax.all_to_all(blocked, 'dap', split_axis=1, concat_axis=0, tiled=True)  17.5 us
    all_to_all x2, starting transfers between devices, return_products(): lax.all_to_all(products, 'dap', split_axis=0, concat_axis=1, tiled=True)  17.5 us
    dot_general x8, matrix products, column_update(): jnp.dot(gated, column_out, preferred_element_type=jnp.float32)  17 us
    all_to_all x2, starting transfers between devices, exchange_parts(): both = lax.all_to_all(both, 'dap', split_axis=1, concat_axis=0, tiled=True)  16.1 us
    dot_general x8, matrix products, column_update(): jnp.einsum('hst,thd->shd', weights, value_rows, preferred_element_type=jn...  15.9 us
  transfers between devices with their start and end apart: 5, of which 5 were waited for; matrix products, arithmetic and copies ran while one was open for 27% of the time, Pallas kernels for 0%

profile of v1, /device:TPU:1, one launch (start us, length us, event | category | flops | bytes accessed | tf_op | source)
XLA Modules:
  0.0 436.3 jit_solution(6235340542201133575)
XLA Ops:
  0.6 3.1 copy.161
  3.7 17.5 %all-to-all-start = ((bf16[4,64,8,256]{3,0,2,1:T(4,128)(2,1)}), bf16[4,64,8,256]{3,0,2,1:T(4,128)(2,1)}, u32[]{:S(2)}, u32[]{:S(2)}) async-start(bf16[4,64,8,256]{3,0,2,1:T(4,128)(2,1)} %bitcast.29), calls=%async_computation | async-start | bytes 2097152 | tf_op jit(solution)/shard_map/all_to_all | solution.py:130
  26.5 46.2 %all-to-all-done = bf16[4,64,8,256]{3,0,2,1:T(4,128)(2,1)} async-done(((bf16[4,64,8,256]{3,0,2,1:T(4,128)(2,1)}), bf16[4,64,8,256]{3,0,2,1:T(4,128)(2,1)}, u32[]{:S(2)}, u32[]{:S(2)}) %all-to-all-start) | async-done | bytes 1048608 | tf_op jit(solution)/shard_map/all_to_all | solution.py:130
  72.7 2.4 copy.162
  78.5 2.8 pad_maximum_fusion
  81.2 8.0 %all-to-all-start.1 = ((bf16[8,64,4,512]{3,0,2,1:T(8,128)(2,1)}), bf16[8,64,4,512]{3,0,2,1:T(8,128)(2,1)S(1)}, u32[]{:S(2)}, u32[]{:S(2)}) async-start(bf16[8,64,4,512]{3,0,2,1:T(8,128)(2,1)} %pad_maximum_fusion), calls=%async_computation.1 | async-start | bytes 4194304 | tf_op jit(solution)/shard_map/all_to_all | solution.py:84
  92.3 59.0 %while.20 = (s32[]{:T(128)}, bf16[4,256,256]{2,1,0:T(8,128)(2,1)}, bf16[4,256,256]{2,1,0:T(8,128)(2,1)}, bf16[2,256,256]{2,1,0:T(8,128)(2,1)}, bf16[2,256,256]{2...) while((s32[]{:T(128)}, bf16[4,256,256]{2,1,0:T(8,128)(2,1)}, ...), condition=%wide.region_7.8_spmd, body=%wide.region_2.7_spmd.sunk | while | flops 274336512 | bytes 4886137 | solution.py:142
  94.4 2.0 fusion.211
  96.4 1.9 convolution_convert_fusion.11
  102.0 2.0 fusion.213
  104.8 2.2 fusion.214
  109.2 2.0 fusion.211
  111.2 1.9 convolution_convert_fusion.11
  116.7 2.0 fusion.213
  119.6 2.2 fusion.214
  123.9 2.0 fusion.211
  125.9 1.9 convolution_convert_fusion.11
  131.5 2.0 fusion.213
  134.3 2.2 fusion.214
  138.7 2.0 fusion.211
  146.2 2.0 fusion.213
  149.1 2.2 fusion.214
  151.3 33.5 %all-to-all-done.1 = bf16[8,64,4,512]{3,0,2,1:T(8,128)(2,1)S(1)} async-done(((bf16[8,64,4,512]{3,0,2,1:T(8,128)(2,1)}), bf16[8,64,4,512]{3,0,2,1:T(8,128)(2,1)S(1)}, u32[]{:S(2)}, u32[]{:S(2)}) %all-to-all-start.1) | async-done | bytes 2097184 | tf_op jit(solution)/shard_map/all_to_all | solution.py:84
  185.8 2.1 copy.169
  187.9 8.6 %all-to-all-start.2 = ((bf16[512,2,512]{2,1,0:T(2,128)(2,1)}), bf16[512,2,512]{2,1,0:T(2,128)(2,1)S(1)}, u32[]{:S(2)}, u32[]{:S(2)}) async-start(bf16[512,2,512]{2,1,0:T(2,128)(2,1)} %copy.169), calls=%async_computation.2 | async-start | bytes 2097152 | tf_op jit(solution)/shard_map/all_to_all | solution.py:90
  196.5 2.8 fusion.127
  199.3 48.7 %all-to-all-done.2 = bf16[512,2,512]{2,1,0:T(2,128)(2,1)S(1)} async-done(((bf16[512,2,512]{2,1,0:T(2,128)(2,1)}), bf16[512,2,512]{2,1,0:T(2,128)(2,1)S(1)}, u32[]{:S(2)}, u32[]{:S(2)}) %all-to-all-start.2) | async-done | bytes 1048608 | tf_op jit(solution)/shard_map/all_to_all | solution.py:90
  253.7 2.0 fusion.87
  255.8 2.7 copy.175
  260.1 3.1 pad_maximum_fusion.1
  263.2 8.1 %all-to-all-start.3 = ((bf16[8,64,4,512]{3,0,2,1:T(8,128)(2,1)}), bf16[8,64,4,512]{3,0,2,1:T(8,128)(2,1)}, u32[]{:S(2)}, u32[]{:S(2)}) async-start(bf16[8,64,4,512]{3,0,2,1:T(8,128)(2,1)} %pad_maximum_fusion.1), calls=%async_computation.3 | async-start | bytes 4194304 | tf_op jit(solution)/shard_map/all_to_all | solution.py:84
  272.5 41.2 %while.21 = (s32[]{:T(128)}, bf16[4,256,256]{2,1,0:T(8,128)(2,1)}, bf16[4,256,256]{2,1,0:T(8,128)(2,1)S(1)}, bf16[2,256,256]{2,1,0:T(8,128)(2,1)}, bf16[2,256,25...) while((s32[]{:T(128)}, bf16[4,256,256]{2,1,0:T(8,128)(2,1)}, ...), condition=%wide.region_17.18_spmd, body=%wide.region_12.17_spmd.sunk | while | flops 274336512 | bytes 5409945 | solution.py:154
  274.1 1.9 convolution_convert_fusion.13
  278.7 2.0 fusion.233
  280.8 2.0 fusion.234
  284.4 1.9 convolution_convert_fusion.13
  289.0 2.0 fusion.233
  291.1 2.0 fusion.234
  294.7 1.9 convolution_convert_fusion.13
  299.3 2.0 fusion.233
  301.4 2.0 fusion.234
  305.0 1.9 convolution_convert_fusion.13
  309.6 2.0 fusion.233
  311.7 2.0 fusion.234
  313.7 53.1 %all-to-all-done.3 = bf16[8,64,4,512]{3,0,2,1:T(8,128)(2,1)} async-done(((bf16[8,64,4,512]{3,0,2,1:T(8,128)(2,1)}), bf16[8,64,4,512]{3,0,2,1:T(8,128)(2,1)}, u32[]{:S(2)}, u32[]{:S(2)}) %all-to-all-start.3) | async-done | bytes 2097184 | tf_op jit(solution)/shard_map/all_to_all | solution.py:84
  369.5 2.1 copy.184
  371.6 8.9 %all-to-all-start.4 = ((bf16[512,2,512]{2,1,0:T(2,128)(2,1)}), bf16[512,2,512]{2,1,0:T(2,128)(2,1)S(1)}, u32[]{:S(2)}, u32[]{:S(2)}) async-start(bf16[512,2,512]{2,1,0:T(2,128)(2,1)} %copy.184), calls=%async_computation.4 | async-start | bytes 2097152 | tf_op jit(solution)/shard_map/all_to_all | solution.py:90
  385.8 46.2 %all-to-all-done.4 = bf16[512,2,512]{2,1,0:T(2,128)(2,1)S(1)} async-done(((bf16[512,2,512]{2,1,0:T(2,128)(2,1)}), bf16[512,2,512]{2,1,0:T(2,128)(2,1)S(1)}, u32[]{:S(2)}, u32[]{:S(2)}) %all-to-all-start.4) | async-done | bytes 1048608 | tf_op jit(solution)/shard_map/all_to_all | solution.py:90
  (164 shorter events, 79.0 us)
Async XLA Ops:
  0.6 20.7 %copy-start.4 = (bf16[8,512,128]{2,1,0:T(8,128)(2,1)S(1)}, bf16[8,512,128]{2,1,0:T(8,128)(2,1)}, u32[]{:S(2)}) copy-start(bf16[8,512,128]{2,1,0:T(8,128)(2,1)} %param.16) | copy-start | bytes 3145732
  3.7 18.1 %copy-start.8 = (s32[512]{0:T(512)S(1)}, s32[512]{0:T(512)}, u32[]{:S(2)}) copy-start(s32[512]{0:T(512)} %param.17) | copy-start | bytes 6148
  3.7 18.1 %copy-start.9 = (s32[512]{0:T(512)S(1)}, s32[512]{0:T(512)}, u32[]{:S(2)}) copy-start(s32[512]{0:T(512)} %param.19) | copy-start | bytes 6148
  3.7 18.3 %copy-start.10 = (f32[2,128]{1,0:T(2,128)S(1)}, f32[2,128]{1,0:T(2,128)}, u32[]{:S(2)}) copy-start(f32[2,128]{1,0:T(2,128)} %param.20) | copy-start | bytes 3076
  3.7 68.9 %all-to-all-start = ((bf16[4,64,8,256]{3,0,2,1:T(4,128)(2,1)}), bf16[4,64,8,256]{3,0,2,1:T(4,128)(2,1)}, u32[]{:S(2)}, u32[]{:S(2)}) async-start(bf16[4,64,8,256]{3,0,2,1:T(4,128)(2,1)} %bitcast.29), calls=%async_computation | async-start | bytes 2097152 | tf_op jit(solution)/shard_map/all_to_all | solution.py:130
  21.3 1.8 copy-start.7
  23.8 1.4 copy-start.6
  76.8 1.7 copy-start.1
  81.2 8.0 %copy-start.11 = (s32[256]{0:T(256)S(1)}, s32[256]{0:T(256)}, u32[]{:S(2)}) copy-start(s32[256]{0:T(256)} %param.18) | copy-start | bytes 3076
  81.2 103.6 %all-to-all-start.1 = ((bf16[8,64,4,512]{3,0,2,1:T(8,128)(2,1)}), bf16[8,64,4,512]{3,0,2,1:T(8,128)(2,1)S(1)}, u32[]{:S(2)}, u32[]{:S(2)}) async-start(bf16[8,64,4,512]{3,0,2,1:T(8,128)(2,1)} %pad_maximum_fusion), calls=%async_computation.1 | async-start | bytes 4194304 | tf_op jit(solution)/shard_map/all_to_all | solution.py:84
  94.4 5.7 %copy-start.12 = (bf16[2,256,256]{2,1,0:T(8,128)(2,1)S(1)}, bf16[2,256,256]{2,1,0:T(8,128)(2,1)}, u32[]{:S(2)}) copy-start(bf16[2,256,256]{2,1,0:T(8,128)(2,1)} %get-tuple-element.267) | copy-start | bytes 786436 | tf_op jit(solution)/shard_map/while
  109.2 5.7 %copy-start.12 = (bf16[2,256,256]{2,1,0:T(8,128)(2,1)S(1)}, bf16[2,256,256]{2,1,0:T(8,128)(2,1)}, u32[]{:S(2)}) copy-start(bf16[2,256,256]{2,1,0:T(8,128)(2,1)} %get-tuple-element.267) | copy-start | bytes 786436 | tf_op jit(solution)/shard_map/while
  123.9 5.7 %copy-start.12 = (bf16[2,256,256]{2,1,0:T(8,128)(2,1)S(1)}, bf16[2,256,256]{2,1,0:T(8,128)(2,1)}, u32[]{:S(2)}) copy-start(bf16[2,256,256]{2,1,0:T(8,128)(2,1)} %get-tuple-element.267) | copy-start | bytes 786436 | tf_op jit(solution)/shard_map/while
  138.7 5.7 %copy-start.12 = (bf16[2,256,256]{2,1,0:T(8,128)(2,1)S(1)}, bf16[2,256,256]{2,1,0:T(8,128)(2,1)}, u32[]{:S(2)}) copy-start(bf16[2,256,256]{2,1,0:T(8,128)(2,1)} %get-tuple-element.267) | copy-start | bytes 786436 | tf_op jit(solution)/shard_map/while
  187.9 60.1 %all-to-all-start.2 = ((bf16[512,2,512]{2,1,0:T(2,128)(2,1)}), bf16[512,2,512]{2,1,0:T(2,128)(2,1)S(1)}, u32[]{:S(2)}, u32[]{:S(2)}) async-start(bf16[512,2,512]{2,1,0:T(2,128)(2,1)} %copy.169), calls=%async_computation.2 | async-start | bytes 2097152 | tf_op jit(solution)/shard_map/all_to_all | solution.py:90
  248.4 0.8 copy-start.14
  248.5 1.6 copy-start.16
  251.5 0.9 copy-start.5
  263.2 8.2 %copy-start = (bf16[4,64,8,256]{3,2,0,1:T(8,128)(2,1)S(1)}, bf16[4,64,8,256]{3,2,0,1:T(8,128)(2,1)}, u32[]{:S(2)}) copy-start(bf16[4,64,8,256]{3,2,0,1:T(8,128)(2,1)} %copy.162) | copy-start | bytes 3145732
  263.2 103.7 %all-to-all-start.3 = ((bf16[8,64,4,512]{3,0,2,1:T(8,128)(2,1)}), bf16[8,64,4,512]{3,0,2,1:T(8,128)(2,1)}, u32[]{:S(2)}, u32[]{:S(2)}) async-start(bf16[8,64,4,512]{3,0,2,1:T(8,128)(2,1)} %pad_maximum_fusion.1), calls=%async_computation.3 | async-start | bytes 4194304 | tf_op jit(solution)/shard_map/all_to_all | solution.py:84
  272.5 5.2 %copy-start.13 = (bf16[2,256,256]{2,1,0:T(8,128)(2,1)S(1)}, bf16[2,256,256]{2,1,0:T(8,128)(2,1)}, u32[]{:S(2)}) copy-start(bf16[2,256,256]{2,1,0:T(8,128)(2,1)} %get-tuple-element.291) | copy-start | bytes 786436 | tf_op jit(solution)/shard_map/while
  274.1 4.6 %copy-start.15 = (bf16[256,256]{0,1:T(8,128)(2,1)}, bf16[256,256]{0,1:T(8,128)(2,1)S(1)}, u32[]{:S(2)}) copy-start(bf16[256,256]{0,1:T(8,128)(2,1)S(1)} %fusion.231) | copy-start | bytes 393220 | tf_op jit(solution)/shard_map/while
  282.8 5.2 %copy-start.13 = (bf16[2,256,256]{2,1,0:T(8,128)(2,1)S(1)}, bf16[2,256,256]{2,1,0:T(8,128)(2,1)}, u32[]{:S(2)}) copy-start(bf16[2,256,256]{2,1,0:T(8,128)(2,1)} %get-tuple-element.291) | copy-start | bytes 786436 | tf_op jit(solution)/shard_map/while
  284.4 4.6 %copy-start.15 = (bf16[256,256]{0,1:T(8,128)(2,1)}, bf16[256,256]{0,1:T(8,128)(2,1)S(1)}, u32[]{:S(2)}) copy-start(bf16[256,256]{0,1:T(8,128)(2,1)S(1)} %fusion.231) | copy-start | bytes 393220 | tf_op jit(solution)/shard_map/while
  293.1 5.2 %copy-start.13 = (bf16[2,256,256]{2,1,0:T(8,128)(2,1)S(1)}, bf16[2,256,256]{2,1,0:T(8,128)(2,1)}, u32[]{:S(2)}) copy-start(bf16[2,256,256]{2,1,0:T(8,128)(2,1)} %get-tuple-element.291) | copy-start | bytes 786436 | tf_op jit(solution)/shard_map/while
  294.7 4.6 %copy-start.15 = (bf16[256,256]{0,1:T(8,128)(2,1)}, bf16[256,256]{0,1:T(8,128)(2,1)S(1)}, u32[]{:S(2)}) copy-start(bf16[256,256]{0,1:T(8,128)(2,1)S(1)} %fusion.231) | copy-start | bytes 393220 | tf_op jit(solution)/shard_map/while
  303.4 5.2 %copy-start.13 = (bf16[2,256,256]{2,1,0:T(8,128)(2,1)S(1)}, bf16[2,256,256]{2,1,0:T(8,128)(2,1)}, u32[]{:S(2)}) copy-start(bf16[2,256,256]{2,1,0:T(8,128)(2,1)} %get-tuple-element.291) | copy-start | bytes 786436 | tf_op jit(solution)/shard_map/while
  305.0 4.6 %copy-start.15 = (bf16[256,256]{0,1:T(8,128)(2,1)}, bf16[256,256]{0,1:T(8,128)(2,1)S(1)}, u32[]{:S(2)}) copy-start(bf16[256,256]{0,1:T(8,128)(2,1)S(1)} %fusion.231) | copy-start | bytes 393220 | tf_op jit(solution)/shard_map/while
  371.6 60.3 %all-to-all-start.4 = ((bf16[512,2,512]{2,1,0:T(2,128)(2,1)}), bf16[512,2,512]{2,1,0:T(2,128)(2,1)S(1)}, u32[]{:S(2)}, u32[]{:S(2)}) async-start(bf16[512,2,512]{2,1,0:T(2,128)(2,1)} %copy.184), calls=%async_computation.4 | async-start | bytes 2097152 | tf_op jit(solution)/shard_map/all_to_all | solution.py:90
  381.9 1.9 copy-start.3
  432.4 1.6 copy-start.2

commit v2 on v1

v2 whole, which is shorter than its diff:
```python
import functools

import jax
import jax.numpy as jnp
from jax import lax
from jax.experimental import pallas as pl
from jax.experimental.pallas import tpu as pltpu
from jax.sharding import PartitionSpec as P

HEADS = 8
HEAD_DIM = 32


EPS = 1e-05


def normalize(values, axis):
    average = jnp.mean(values, axis=axis, keepdims=True)
    centered = values - average
    variance = jnp.mean(centered * centered, axis=axis, keepdims=True)
    return centered * lax.rsqrt(variance + EPS)


def column_update(column, key_bias, score_proj, value_gate, column_out):
    count = column.shape[0]
    normed = normalize(column.astype(jnp.float32), 1).astype(jnp.bfloat16)
    queries = (
        jnp.dot(normed, score_proj[0], preferred_element_type=jnp.float32) * HEAD_DIM ** (-0.5)
    ).astype(jnp.bfloat16)
    key_rows = jnp.dot(normed, score_proj[1], preferred_element_type=jnp.float32).astype(
        jnp.bfloat16
    )
    value_rows = jnp.dot(normed, value_gate[0], preferred_element_type=jnp.float32).astype(
        jnp.bfloat16
    )
    gate_rows = jax.nn.sigmoid(jnp.dot(normed, value_gate[1], preferred_element_type=jnp.float32))
    queries = queries.reshape(count, HEADS, HEAD_DIM)
    key_rows = key_rows.reshape(count, HEADS, HEAD_DIM)
    value_rows = value_rows.reshape(count, HEADS, HEAD_DIM)
    scores = (
        jnp.einsum("shd,thd->hst", queries, key_rows, preferred_element_type=jnp.float32)
        + key_bias[None, None, :]
    )
    highest = jnp.max(scores, axis=-1, keepdims=True)
    raised = jnp.exp(scores - highest)
    weights = (raised / jnp.sum(raised, axis=-1, keepdims=True)).astype(jnp.bfloat16)
    mixture = jnp.einsum(
        "hst,thd->shd", weights, value_rows, preferred_element_type=jnp.float32
    ).reshape(count, HEADS * HEAD_DIM)
    gated = (gate_rows * mixture).astype(jnp.bfloat16)
    return (
        column.astype(jnp.float32) + jnp.dot(gated, column_out, preferred_element_type=jnp.float32)
    ).astype(jnp.bfloat16)


LANES = 128


def tiled(shape):
    return (shape[1] // LANES, shape[0], LANES)


def collect(staged, parts):
    for tile in range(staged.shape[0]):
        parts[:, tile * LANES : (tile + 1) * LANES] = staged[tile].astype(parts.dtype)


def scale_rows(values):
    average = jnp.mean(values, axis=0, keepdims=True)
    centered = values - average
    variance = jnp.mean(centered * centered, axis=0, keepdims=True)
    return (centered * lax.rsqrt(variance + EPS)).astype(jnp.bfloat16)


def project_row(row, pair_sum, pair_mask, weights, staged):
    sides = 2 * pair_sum.shape[0]
    rows = staged.shape[1] // sides
    projected = jnp.dot(weights, scale_rows(pair_sum), preferred_element_type=jnp.float32)
    parts = jax.nn.sigmoid(projected[:sides]) * projected[sides : 2 * sides] * pair_mask
    for tile in range(staged.shape[0]):
        staged[tile, pl.ds(row, sides, stride=rows), :] = parts[:, tile * LANES : (tile + 1) * LANES]
    return jax.nn.sigmoid(projected[2 * sides :])


def open_kernel(pair_act, same_chain, pair_mask, embed, weights, parts, pair_sum, gate, staged):
    for row in range(pair_act.shape[0]):
        channels = pair_act[row].astype(jnp.float32).T
        channels += jnp.where(same_chain[row : row + 1, :] > 0, embed[:, 0:1], embed[:, 1:2])
        pair_sum[row] = channels
        gate[row] = project_row(
            row, channels, pair_mask[row : row + 1, :], weights[...], staged
        )
    collect(staged, parts)


def update_row(row, pair_sum, products, gate, weights):
    rows = pair_sum.shape[0]
    width = products.shape[1] // rows
    tiles = [products[tile, pl.ds(row, width, stride=rows), :] for tile in range(products.shape[0])]
    normed = scale_rows(jnp.concatenate(tiles, axis=1))
    update = jnp.dot(weights, normed, preferred_element_type=jnp.float32)
    return pair_sum[row] + gate[row] * update


def middle_kernel(
    products, pair_sum, gate, pair_mask, weights_out, weights, parts, pair_next, gate_next, wide, staged
):
    for tile in range(wide.shape[0]):
        wide[tile] = products[:, tile * LANES : (tile + 1) * LANES].astype(jnp.float32)
    for row in range(pair_sum.shape[0]):
        channels = update_row(row, pair_sum, wide, gate, weights_out[...])
        pair_next[row] = channels
        gate_next[row] = project_row(
            row, channels, pair_mask[row : row + 1, :], weights[...], staged
        )
    collect(staged, parts)


def close_kernel(products, pair_sum, gate, weights_out, pair_new, wide):
    for tile in range(wide.shape[0]):
        wide[tile] = products[:, tile * LANES : (tile + 1) * LANES].astype(jnp.float32)
    for row in range(pair_sum.shape[0]):
        channels = update_row(row, pair_sum, wide, gate, weights_out[...])
        pair_new[row] = channels.T.astype(pair_new.dtype)


KERNEL = pltpu.CompilerParams(vmem_limit_bytes=40 * 1024 * 1024)


def open_pair(pair_act, same_chain, pair_mask, embed, weights):
    rows, side, channels = pair_act.shape
    flat = (2 * channels * rows, side)
    wide = jax.ShapeDtypeStruct((rows, channels, side), jnp.float32)
    return pl.pallas_call(
        open_kernel,
        out_shape=(jax.ShapeDtypeStruct(flat, jnp.bfloat16), wide, wide),
        scratch_shapes=[pltpu.VMEM(tiled(flat), jnp.float32)],
        compiler_params=KERNEL,
    )(pair_act, same_chain, pair_mask, embed, weights)


def middle_pair(products, pair_sum, gate, pair_mask, weights_out, weights):
    rows, channels, side = pair_sum.shape
    flat = (2 * channels * rows, side)
    wide = jax.ShapeDtypeStruct((rows, channels, side), jnp.float32)
    return pl.pallas_call(
        middle_kernel,
        out_shape=(jax.ShapeDtypeStruct(flat, jnp.bfloat16), wide, wide),
        scratch_shapes=[pltpu.VMEM(tiled(products.shape), jnp.float32), pltpu.VMEM(tiled(flat), jnp.float32)],
        compiler_params=KERNEL,
    )(products, pair_sum, gate, pair_mask, weights_out, weights)


def close_pair(products, pair_sum, gate, weights_out):
    rows, channels, side = pair_sum.shape
    return pl.pallas_call(
        close_kernel,
        out_shape=jax.ShapeDtypeStruct((rows, side, channels), jnp.bfloat16),
        scratch_shapes=[pltpu.VMEM(tiled(products.shape), jnp.float32)],
        compiler_params=KERNEL,
    )(products, pair_sum, gate, weights_out)


def order_weights(weights_in, width, devices):
    share = width // devices
    depth = weights_in.shape[0]
    groups = [
        weights_in[:, step * width : (step + 1) * width].T.reshape(devices, share, depth)
        for step in range(4)
    ]
    gates = jnp.concatenate([groups[0], groups[2]], axis=1).reshape(2 * width, depth)
    values = jnp.concatenate([groups[1], groups[3]], axis=1).reshape(2 * width, depth)
    return jnp.concatenate([gates, values, weights_in[:, 4 * width :].T])


def exchange(flat, devices):
    blocks = flat.reshape(devices, flat.shape[0] // devices, flat.shape[1])
    return lax.all_to_all(blocks, "dap", split_axis=0, concat_axis=0, tiled=True)


def split_parts(both, share, rows):
    devices, held, side = both.shape
    both = both.reshape(devices, 2, share, rows, side)
    return both[:, 0], both[:, 1]


def return_products(products, devices):
    share, side, _ = products.shape
    blocks = products.reshape(share, devices, side // devices, side)
    blocks = jnp.moveaxis(blocks, 0, 1).reshape(devices, -1, side)
    got = lax.all_to_all(blocks, "dap", split_axis=0, concat_axis=0, tiled=True)
    return got.reshape(-1, side)


def on_device(
    alignment,
    pair_act,
    crop_mask,
    seq_mask,
    chain_ids,
    chain_embed,
    score_proj,
    value_gate,
    column_out,
    triangle_in,
    triangle_out,
):
    rows_here = pair_act.shape[0]
    width = triangle_out.shape[1]
    devices = lax.axis_size("dap")
    row_start = lax.axis_index("dap") * rows_here
    share = width // devices
    seq_here = alignment.shape[0]
    blocked = alignment.reshape(seq_here, devices, rows_here, alignment.shape[2])
    blocked = lax.all_to_all(blocked, "dap", split_axis=1, concat_axis=0, tiled=True)
    by_column = jnp.moveaxis(blocked[:, 0], 1, 0)

    kept_rows = jnp.maximum(seq_mask, (jnp.arange(seq_mask.shape[0]) == 0).astype(jnp.int32))
    key_bias = (kept_rows - 1).astype(jnp.float32) * 1000000000.0
    crop = crop_mask.astype(jnp.float32)
    crop_rows = lax.dynamic_slice_in_dim(crop, row_start, rows_here)
    pair_mask = crop_rows[:, None] * crop[None, :]
    chain_rows = lax.dynamic_slice_in_dim(chain_ids, row_start, rows_here)
    same_chain = (chain_rows[:, None] == chain_ids[None, :]).astype(jnp.float32)
    ordered = [order_weights(triangle_in[step], width, devices) for step in range(2)]
    turned = [triangle_out[step].T for step in range(2)]

    attend = functools.partial(
        lax.map,
        lambda column: column_update(column, key_bias, score_proj, value_gate, column_out),
    )
    parts, pair_sum, gate = open_pair(
        pair_act, same_chain, pair_mask, chain_embed.T, ordered[0]
    )
    parts, blocked = lax.optimization_barrier((parts, blocked))
    by_column = jnp.moveaxis(blocked[:, 0], 1, 0)
    both = exchange(parts, devices)
    half = rows_here // 2
    first = attend(by_column[:half])
    both, first = lax.optimization_barrier((both, first))
    left, right = split_parts(both, share, rows_here)
    left = jnp.moveaxis(left, 1, 0).reshape(share, -1, left.shape[-1])
    right = jnp.moveaxis(right, 1, 0).reshape(share, -1, right.shape[-1])
    products = jnp.einsum(
        "cik,cjk->cij", left, right, preferred_element_type=jnp.float32
    ).astype(jnp.bfloat16)
    products = return_products(products, devices)
    parts, pair_sum, gate = middle_pair(
        products, pair_sum, gate, pair_mask, turned[0], ordered[1]
    )
    parts, blocked = lax.optimization_barrier((parts, blocked))
    by_column = jnp.moveaxis(blocked[:, 0], 1, 0)
    both = exchange(parts, devices)
    second = attend(by_column[half:])
    both, second = lax.optimization_barrier((both, second))
    left, right = split_parts(both, share, rows_here)
    left = jnp.moveaxis(left, 1, 0).reshape(share, -1, left.shape[-1])
    right = jnp.moveaxis(right, 1, 0).reshape(share, -1, right.shape[-1])
    products = jnp.einsum(
        "cki,ckj->cij", left, right, preferred_element_type=jnp.float32
    ).astype(jnp.bfloat16)
    products = return_products(products, devices)
    attended = jnp.moveaxis(jnp.concatenate([first, second]), 0, 1)
    alignment_new = attended.reshape(attended.shape[0], rows_here, alignment.shape[2])
    pair_new = close_pair(products, pair_sum, gate, turned[1])
    return (alignment_new, pair_new)


def solution(mesh):
    placed = (
        P(("dp", "dap"), None, None),
        P(("dp", "dap"), None, None),
        P("dp"),
        P("dp"),
        P("dp"),
        P(),
        P(),
        P(),
        P(),
        P(),
        P(),
    )
    return jax.shard_map(
        on_device,
        mesh=mesh,
        in_specs=placed,
        out_specs=(P("dp", "dap", None), P(("dp", "dap"), None, None)),
        check_vma=False,
    )
```

time: 438 us -> 423 us (0.966)
  waiting for transfers between devices: 228 us -> 255 us
  matrix products: 97.6 us -> 72.7 us
  other arithmetic: 23.1 us -> 4.4 us
  Pallas kernels: 0 us -> 11.5 us
  local copies, waits for them, and re-layouts: 35.5 us -> 25.9 us
    all_to_all x4, waiting for transfers between devices: 181 us -> 212 us  [the longest x2 114 us: exchange(): lax.all_to_all(blocks, 'dap', split_axis=0, concat_axis=0, tiled=True)]
    pallas_call x0 -> x3, Pallas kernels: none -> 11.5 us  [the longest x1 4.55 us: middle_pair(): pl.pallas_call(middle_kernel, out_shape=(jax.ShapeDtypeStruct(flat, jnp.b...]
    dot_general x8 -> x2, matrix products: 11.4 us -> 1.51 us  [the longest x1 0.76 us: on_device(): jnp.einsum('cki,ckj->cij', left, right, preferred_element_type=jnp.float32)]
    optimization_barrier x4 -> x0, local copies, waits for them, and re-layouts: 7.75 us -> none  [on_device(): lax.optimization_barrier((left_part, right_part, by_column))]
    unnamed x31 -> x40, local copies, waits for them, and re-layouts: 7.96 us -> 13.8 us
    concatenate x2 -> x6, other arithmetic: 5.83 us -> 0.32 us  [the longest x2 0.15 us: order_weights(): jnp.concatenate([groups[0], groups[2]], axis=1).reshape(2 * width, depth)]
    reduce_sum x12 -> x8, other arithmetic: 6.55 us -> 1.46 us  [normalize(): variance = jnp.mean(centered * centered, axis=axis, keepdims=True)]
    convert_element_type x4 -> x0, local copies, waits for them, and re-layouts: 4.45 us -> none  [the longest x1 2.1 us: on_device(): products = jnp.einsum('ick,jck->icj', both[:, :share], both[:, share:], p...]
  transfers between devices with their start and end apart: 5 -> 5, of which waited for: 5 -> 5; matrix products, arithmetic and copies ran while one was open for 27% -> 20% of each run, Pallas kernels for 0% -> 1%
where the time goes in v2:
time: 423 us; the launch traced here: 422 us
  waiting for transfers between devices  255 us (60%)
  matrix products  72.7 us (17%)
  starting transfers between devices  50.9 us (12%)
  local copies, waits for them, and re-layouts  25.9 us (6%)
  Pallas kernels  11.5 us (3%)
  other arithmetic  4.4 us (1%)
    all_to_all x2, waiting for transfers between devices, exchange(): lax.all_to_all(blocks, 'dap', split_axis=0, concat_axis=0, tiled=True)  114 us
    all_to_all x2, waiting for transfers between devices, return_products(): got = lax.all_to_all(blocks, 'dap', split_axis=0, concat_axis=0, tiled=True)  97.9 us
    all_to_all x1, waiting for transfers between devices, on_device(): lax.all_to_all(blocked, 'dap', split_axis=1, concat_axis=0, tiled=True)  43.3 us
    all_to_all x1, starting transfers between devices, on_device(): lax.all_to_all(blocked, 'dap', split_axis=1, concat_axis=0, tiled=True)  17.5 us
    all_to_all x2, starting transfers between devices, return_products(): got = lax.all_to_all(blocks, 'dap', split_axis=0, concat_axis=0, tiled=True)  17.3 us
    all_to_all x2, starting transfers between devices, exchange(): lax.all_to_all(blocks, 'dap', split_axis=0, concat_axis=0, tiled=True)  16.1 us
    dot_general x8, matrix products, column_update(): jnp.dot(gated, column_out, preferred_element_type=jnp.float32)  15.7 us
    dot_general x8, matrix products, column_update(): jnp.einsum('hst,thd->shd', weights, value_rows, preferred_element_type=jn...  15.6 us
  transfers between devices with their start and end apart: 5, of which 5 were waited for; matrix products, arithmetic and copies ran while one was open for 20% of the time, Pallas kernels for 1%

profile of v2, /device:TPU:1, one launch (start us, length us, event | category | flops | bytes accessed | tf_op | source)
XLA Modules:
  0.0 421.6 jit_solution(7635636975928042878)
XLA Ops:
  0.7 3.0 copy.107
  3.7 17.5 %all-to-all-start = ((bf16[4,64,8,256]{3,0,2,1:T(4,128)(2,1)}), bf16[4,64,8,256]{3,0,2,1:T(4,128)(2,1)}, u32[]{:S(2)}, u32[]{:S(2)}) async-start(bf16[4,64,8,256]{3,0,2,1:T(4,128)(2,1)} %bitcast.37), calls=%async_computation | async-start | bytes 2097152 | tf_op jit(solution)/shard_map/all_to_all | solution.py:215
  22.1 4.5 %shard_map.122 = (bf16[2048,512]{1,0:T(8,128)(2,1)}, f32[8,128,512]{2,1,0:T(8,128)S(1)}, f32[8,128,512]{2,1,0:T(8,128)S(1)}) custom-call(bf16[8,512,128]{2,1,0:T(8,128)(2,1)S(1)} %copy-done.7, f32[8,512]{1,0:T(8,128)S(1)} %compare_convert_fusion.same_chain, f32[8,512]{1,0:T(8,128)S(1)} %broadcast_multiply_fusion.2.pair_mask, f32[128,2]{1,0:T(8,128)S(1)} %bitcast.282, ...), custom_call_target="tpu_custom_call" | custom-call | tf_op jit(solution)/shard_map/pallas_call | solution.py:134
  29.3 43.3 %all-to-all-done = bf16[4,64,8,256]{3,0,2,1:T(4,128)(2,1)} async-done(((bf16[4,64,8,256]{3,0,2,1:T(4,128)(2,1)}), bf16[4,64,8,256]{3,0,2,1:T(4,128)(2,1)}, u32[]{:S(2)}, u32[]{:S(2)}) %all-to-all-start) | async-done | bytes 1048608 | tf_op jit(solution)/shard_map/all_to_all | solution.py:215
  72.6 1.4 copy.108
  74.1 8.0 %all-to-all-start.1 = ((bf16[64,32,512]{2,1,0:T(8,128)(2,1)}), bf16[64,32,512]{2,1,0:T(8,128)(2,1)S(1)}, u32[]{:S(2)}, u32[]{:S(2)}) async-start(bf16[64,32,512]{2,1,0:T(8,128)(2,1)} %bitcast.41), calls=%async_computation.1 | async-start | bytes 4194304 | tf_op jit(solution)/shard_map/all_to_all | solution.py:178
  83.2 40.9 %while.20 = (s32[]{:T(128)}, bf16[4,256,256]{2,1,0:T(8,128)(2,1)}, bf16[4,256,256]{2,1,0:T(8,128)(2,1)S(1)}, bf16[2,256,256]{2,1,0:T(8,128)(2,1)}, bf16[2,256,25...) while((s32[]{:T(128)}, bf16[4,256,256]{2,1,0:T(8,128)(2,1)}, ...), condition=%wide.region_5.6_spmd, body=%wide.region_0.5_spmd.sunk | while | flops 274336512 | bytes 5409945 | solution.py:239
  84.8 1.9 convolution_convert_fusion.11
  86.7 1.7 fusion.172
  89.3 2.0 fusion.173
  91.5 1.9 fusion.174
  95.0 1.9 convolution_convert_fusion.11
  96.9 1.7 fusion.172
  99.6 2.0 fusion.173
  101.7 2.0 fusion.174
  105.2 1.9 convolution_convert_fusion.11
  107.1 1.7 fusion.172
  109.8 2.0 fusion.173
  111.9 1.9 fusion.174
  115.4 1.9 convolution_convert_fusion.11
  117.3 1.7 fusion.172
  120.0 2.0 fusion.173
  122.1 2.0 fusion.174
  124.1 53.6 %all-to-all-done.1 = bf16[64,32,512]{2,1,0:T(8,128)(2,1)S(1)} async-done(((bf16[64,32,512]{2,1,0:T(8,128)(2,1)}), bf16[64,32,512]{2,1,0:T(8,128)(2,1)S(1)}, u32[]{:S(2)}, u32[]{:S(2)}) %all-to-all-start.1) | async-done | bytes 2097184 | tf_op jit(solution)/shard_map/all_to_all | solution.py:178
  179.7 8.6 %all-to-all-start.2 = ((bf16[64,16,512]{2,1,0:T(8,128)(2,1)}), bf16[64,16,512]{2,1,0:T(8,128)(2,1)S(1)}, u32[]{:S(2)}, u32[]{:S(2)}) async-start(bf16[64,16,512]{2,1,0:T(8,128)(2,1)} %bitcast.194), calls=%async_computation.2 | async-start | bytes 2097152 | tf_op jit(solution)/shard_map/all_to_all | solution.py:191
  188.9 50.9 %all-to-all-done.2 = bf16[64,16,512]{2,1,0:T(8,128)(2,1)S(1)} async-done(((bf16[64,16,512]{2,1,0:T(8,128)(2,1)}), bf16[64,16,512]{2,1,0:T(8,128)(2,1)S(1)}, u32[]{:S(2)}, u32[]{:S(2)}) %all-to-all-start.2) | async-done | bytes 1048608 | tf_op jit(solution)/shard_map/all_to_all | solution.py:191
  239.8 1.6 copy-done.4
  241.4 1.6 copy-done.6
  243.0 4.6 %shard_map.123 = (bf16[2048,512]{1,0:T(8,128)(2,1)S(1)}, f32[8,128,512]{2,1,0:T(8,128)S(1)}, f32[8,128,512]{2,1,0:T(8,128)S(1)}) custom-call(bf16[1024,512]{1,0:T(8,128)(2,1)S(1)} %bitcast.279, f32[8,128,512]{2,1,0:T(8,128)S(1)} %copy-done.4, f32[8,128,512]{2,1,0:T(8,128)S(1)} %copy-done.6, f32[8,512]{1,0:T(8,128)S(1)} %broadcast_multiply_fusion.2.pair_mask, ...), custom_call_target="tpu_custom_call" | custom-call | tf_op jit(solution)/shard_map/pallas_call | solution.py:146
  250.2 8.1 %all-to-all-start.3 = ((bf16[64,32,512]{2,1,0:T(8,128)(2,1)}), bf16[64,32,512]{2,1,0:T(8,128)(2,1)}, u32[]{:S(2)}, u32[]{:S(2)}) async-start(bf16[64,32,512]{2,1,0:T(8,128)(2,1)} %bitcast.281), calls=%async_computation.3 | async-start | bytes 4194304 | tf_op jit(solution)/shard_map/all_to_all | solution.py:178
  259.6 34.2 %while.21 = (s32[]{:T(128)}, bf16[4,256,256]{2,1,0:T(8,128)(2,1)}, bf16[4,256,256]{2,1,0:T(8,128)(2,1)S(1)}, bf16[2,256,256]{2,1,0:T(8,128)(2,1)}, bf16[2,256,25...) while((s32[]{:T(128)}, bf16[4,256,256]{2,1,0:T(8,128)(2,1)}, ...), condition=%wide.region_11.12_spmd, body=%wide.region_6.11_spmd.sunk | while | flops 274336512 | bytes 5409945 | solution.py:254
  264.1 1.9 fusion.193
  266.2 2.0 fusion.194
  272.7 1.9 fusion.193
  274.8 2.0 fusion.194
  281.3 1.9 fusion.193
  283.3 2.0 fusion.194
  289.8 1.9 fusion.193
  291.9 2.0 fusion.194
  293.8 60.1 %all-to-all-done.3 = bf16[64,32,512]{2,1,0:T(8,128)(2,1)} async-done(((bf16[64,32,512]{2,1,0:T(8,128)(2,1)}), bf16[64,32,512]{2,1,0:T(8,128)(2,1)}, u32[]{:S(2)}, u32[]{:S(2)}) %all-to-all-start.3) | async-done | bytes 2097184 | tf_op jit(solution)/shard_map/all_to_all | solution.py:178
  353.9 1.7 slice_bitcast_fusion.1
  357.5 8.6 %all-to-all-start.4 = ((bf16[64,16,512]{2,1,0:T(8,128)(2,1)}), bf16[64,16,512]{2,1,0:T(8,128)(2,1)S(1)}, u32[]{:S(2)}, u32[]{:S(2)}) async-start(bf16[64,16,512]{2,1,0:T(8,128)(2,1)} %bitcast.290), calls=%async_computation.4 | async-start | bytes 2097152 | tf_op jit(solution)/shard_map/all_to_all | solution.py:191
  366.2 1.5 copy.116
  367.7 1.5 copy.117
  369.2 1.5 maximum_bitcast_fusion
  370.6 46.9 %all-to-all-done.4 = bf16[64,16,512]{2,1,0:T(8,128)(2,1)S(1)} async-done(((bf16[64,16,512]{2,1,0:T(8,128)(2,1)}), bf16[64,16,512]{2,1,0:T(8,128)(2,1)S(1)}, u32[]{:S(2)}, u32[]{:S(2)}) %all-to-all-start.4) | async-done | bytes 1048608 | tf_op jit(solution)/shard_map/all_to_all | solution.py:191
  417.6 1.6 copy-done.1
  419.2 2.4 shard_map.124
  (159 shorter events, 41.9 us)
Async XLA Ops:
  0.6 20.6 %copy-start.10 = (bf16[2,128,640]{2,1,0:T(8,128)(2,1)S(1)}, bf16[2,128,640]{2,1,0:T(8,128)(2,1)}, u32[]{:S(2)}) copy-start(bf16[2,128,640]{2,1,0:T(8,128)(2,1)} %param.24) | copy-start | bytes 983044
  0.6 20.8 %copy-start.13 = (s32[512]{0:T(512)S(1)}, s32[512]{0:T(512)}, u32[]{:S(2)}) copy-start(s32[512]{0:T(512)} %param.17) | copy-start | bytes 6148
  0.7 20.9 %copy-start.12 = (s32[512]{0:T(512)S(1)}, s32[512]{0:T(512)}, u32[]{:S(2)}) copy-start(s32[512]{0:T(512)} %param.19) | copy-start | bytes 6148
  0.7 21.0 %copy-start.14 = (f32[2,128]{1,0:T(2,128)S(1)}, f32[2,128]{1,0:T(2,128)}, u32[]{:S(2)}) copy-start(f32[2,128]{1,0:T(2,128)} %param.20) | copy-start | bytes 3076
  3.7 18.4 %copy-start.7 = (bf16[8,512,128]{2,1,0:T(8,128)(2,1)S(1)}, bf16[8,512,128]{2,1,0:T(8,128)(2,1)}, u32[]{:S(2)}) copy-start(bf16[8,512,128]{2,1,0:T(8,128)(2,1)} %pair_act.1) | copy-start | bytes 3145732
  3.7 68.9 %all-to-all-start = ((bf16[4,64,8,256]{3,0,2,1:T(4,128)(2,1)}), bf16[4,64,8,256]{3,0,2,1:T(4,128)(2,1)}, u32[]{:S(2)}, u32[]{:S(2)}) async-start(bf16[4,64,8,256]{3,0,2,1:T(4,128)(2,1)} %bitcast.37), calls=%async_computation | async-start | bytes 2097152 | tf_op jit(solution)/shard_map/all_to_all | solution.py:215
  26.7 1.3 copy-start.3
  28.0 1.3 copy-start.5
  74.1 8.0 %copy-start.8 = (bf16[4,64,8,256]{3,2,0,1:T(8,128)(2,1)}, bf16[4,64,8,256]{3,2,0,1:T(8,128)(2,1)S(1)}, u32[]{:S(2)}) copy-start(bf16[4,64,8,256]{3,2,0,1:T(8,128)(2,1)S(1)} %copy.108) | copy-start | bytes 3145732
  74.1 8.0 %copy-start.15 = (s32[256]{0:T(256)S(1)}, s32[256]{0:T(256)}, u32[]{:S(2)}) copy-start(s32[256]{0:T(256)} %param.18) | copy-start | bytes 3076
  74.1 103.6 %all-to-all-start.1 = ((bf16[64,32,512]{2,1,0:T(8,128)(2,1)}), bf16[64,32,512]{2,1,0:T(8,128)(2,1)S(1)}, u32[]{:S(2)}, u32[]{:S(2)}) async-start(bf16[64,32,512]{2,1,0:T(8,128)(2,1)} %bitcast.41), calls=%async_computation.1 | async-start | bytes 4194304 | tf_op jit(solution)/shard_map/all_to_all | solution.py:178
  82.1 1.1 copy-start.18
  83.2 5.1 %copy-start.16 = (bf16[2,256,256]{2,1,0:T(8,128)(2,1)S(1)}, bf16[2,256,256]{2,1,0:T(8,128)(2,1)}, u32[]{:S(2)}) copy-start(bf16[2,256,256]{2,1,0:T(8,128)(2,1)} %get-tuple-element.271) | copy-start | bytes 786436 | tf_op jit(solution)/shard_map/while
  84.8 4.6 %copy-start.19 = (bf16[256,256]{0,1:T(8,128)(2,1)}, bf16[256,256]{0,1:T(8,128)(2,1)S(1)}, u32[]{:S(2)}) copy-start(bf16[256,256]{0,1:T(8,128)(2,1)S(1)} %fusion.171) | copy-start | bytes 393220 | tf_op jit(solution)/shard_map/while
  93.4 5.1 %copy-start.16 = (bf16[2,256,256]{2,1,0:T(8,128)(2,1)S(1)}, bf16[2,256,256]{2,1,0:T(8,128)(2,1)}, u32[]{:S(2)}) copy-start(bf16[2,256,256]{2,1,0:T(8,128)(2,1)} %get-tuple-element.271) | copy-start | bytes 786436 | tf_op jit(solution)/shard_map/while
  95.0 4.6 %copy-start.19 = (bf16[256,256]{0,1:T(8,128)(2,1)}, bf16[256,256]{0,1:T(8,128)(2,1)S(1)}, u32[]{:S(2)}) copy-start(bf16[256,256]{0,1:T(8,128)(2,1)S(1)} %fusion.171) | copy-start | bytes 393220 | tf_op jit(solution)/shard_map/while
  103.6 5.1 %copy-start.16 = (bf16[2,256,256]{2,1,0:T(8,128)(2,1)S(1)}, bf16[2,256,256]{2,1,0:T(8,128)(2,1)}, u32[]{:S(2)}) copy-start(bf16[2,256,256]{2,1,0:T(8,128)(2,1)} %get-tuple-element.271) | copy-start | bytes 786436 | tf_op jit(solution)/shard_map/while
  105.2 4.6 %copy-start.19 = (bf16[256,256]{0,1:T(8,128)(2,1)}, bf16[256,256]{0,1:T(8,128)(2,1)S(1)}, u32[]{:S(2)}) copy-start(bf16[256,256]{0,1:T(8,128)(2,1)S(1)} %fusion.171) | copy-start | bytes 393220 | tf_op jit(solution)/shard_map/while
  113.9 5.1 %copy-start.16 = (bf16[2,256,256]{2,1,0:T(8,128)(2,1)S(1)}, bf16[2,256,256]{2,1,0:T(8,128)(2,1)}, u32[]{:S(2)}) copy-start(bf16[2,256,256]{2,1,0:T(8,128)(2,1)} %get-tuple-element.271) | copy-start | bytes 786436 | tf_op jit(solution)/shard_map/while
  115.4 4.6 %copy-start.19 = (bf16[256,256]{0,1:T(8,128)(2,1)}, bf16[256,256]{0,1:T(8,128)(2,1)S(1)}, u32[]{:S(2)}) copy-start(bf16[256,256]{0,1:T(8,128)(2,1)S(1)} %fusion.171) | copy-start | bytes 393220 | tf_op jit(solution)/shard_map/while
  178.6 9.9 %copy-start.11 = (bf16[2,128,128]{2,1,0:T(8,128)(2,1)S(1)}, bf16[2,128,128]{2,1,0:T(8,128)(2,1)}, u32[]{:S(2)}) copy-start(bf16[2,128,128]{2,1,0:T(8,128)(2,1)} %param.25) | copy-start | bytes 196612
  179.7 60.1 %all-to-all-start.2 = ((bf16[64,16,512]{2,1,0:T(8,128)(2,1)}), bf16[64,16,512]{2,1,0:T(8,128)(2,1)S(1)}, u32[]{:S(2)}, u32[]{:S(2)}) async-start(bf16[64,16,512]{2,1,0:T(8,128)(2,1)} %bitcast.194), calls=%async_computation.2 | async-start | bytes 2097152 | tf_op jit(solution)/shard_map/all_to_all | solution.py:191
  239.8 1.6 copy-start.4
  241.4 1.6 copy-start.6
  247.6 1.3 copy-start
  248.9 1.3 copy-start.2
  250.2 8.2 %copy-start.9 = (bf16[4,64,8,256]{3,2,0,1:T(8,128)(2,1)S(1)}, bf16[4,64,8,256]{3,2,0,1:T(8,128)(2,1)}, u32[]{:S(2)}) copy-start(bf16[4,64,8,256]{3,2,0,1:T(8,128)(2,1)} %copy-done.8) | copy-start | bytes 3145732
  250.2 103.7 %all-to-all-start.3 = ((bf16[64,32,512]{2,1,0:T(8,128)(2,1)}), bf16[64,32,512]{2,1,0:T(8,128)(2,1)}, u32[]{:S(2)}, u32[]{:S(2)}) async-start(bf16[64,32,512]{2,1,0:T(8,128)(2,1)} %bitcast.281), calls=%async_computation.3 | async-start | bytes 4194304 | tf_op jit(solution)/shard_map/all_to_all | solution.py:178
  259.6 3.6 copy-start.17
  262.4 1.8 copy-start.20
  268.2 3.6 copy-start.17
  270.9 1.8 copy-start.20
  276.7 3.6 copy-start.17
  279.5 1.8 copy-start.20
  285.3 3.6 copy-start.17
  288.0 1.8 copy-start.20
  357.5 60.1 %all-to-all-start.4 = ((bf16[64,16,512]{2,1,0:T(8,128)(2,1)}), bf16[64,16,512]{2,1,0:T(8,128)(2,1)S(1)}, u32[]{:S(2)}, u32[]{:S(2)}) async-start(bf16[64,16,512]{2,1,0:T(8,128)(2,1)} %bitcast.290), calls=%async_computation.4 | async-start | bytes 2097152 | tf_op jit(solution)/shard_map/all_to_all | solution.py:191
  417.6 1.6 copy-start.1

commit v3 on v0

v3 whole, which is shorter than its diff:
```python
import jax
import jax.numpy as jnp
from jax import lax
from jax.experimental import pallas as pl
from jax.experimental.pallas import tpu as pltpu
from jax.sharding import PartitionSpec as P

HEADS = 8
HEAD_DIM = 32


EPS = 1e-05


def normalize(values, axis):
    average = jnp.mean(values, axis=axis, keepdims=True)
    centered = values - average
    variance = jnp.mean(centered * centered, axis=axis, keepdims=True)
    return centered * lax.rsqrt(variance + EPS)


LANES = 128


def collect(staged, parts):
    sides, tiles, _, lanes = staged.shape
    held = parts.shape[1] // sides
    for side in range(sides):
        for tile in range(tiles):
            piece = staged[side, tile].reshape(parts.shape[0], held, lanes)
            parts[:, side * held : (side + 1) * held, tile * lanes : (tile + 1) * lanes] = (
                piece.astype(parts.dtype)
            )


def scale_rows(values):
    average = jnp.mean(values, axis=0, keepdims=True)
    centered = values - average
    variance = jnp.mean(centered * centered, axis=0, keepdims=True)
    return (centered * lax.rsqrt(variance + EPS)).astype(jnp.bfloat16)


def turn(values):
    return values.astype(jnp.float32).T.astype(values.dtype)


def project(normed, weights):
    return jnp.dot(weights, normed, preferred_element_type=jnp.float32)


def stage_row(row, rows, channels, weights, mask, staged):
    projected = project(scale_rows(channels), weights)
    width = staged.shape[2] // rows
    for side in range(2):
        gates, values = (
            projected[step * width : (step + 1) * width] for step in (2 * side, 2 * side + 1)
        )
        parts = jax.nn.sigmoid(gates) * values * mask
        for tile in range(staged.shape[1]):
            staged[side, tile, pl.ds(row, width, stride=rows), :] = parts[
                :, tile * LANES : (tile + 1) * LANES
            ]


def widen(products, wide):
    devices, held, lanes = products.shape
    held = held * lanes // (wide.shape[0] * LANES)
    for tile in range(wide.shape[0]):
        half, lane = divmod(tile * LANES, lanes)
        piece = products[:, half * held : (half + 1) * held, lane : lane + LANES]
        wide[tile] = piece.astype(jnp.float32).reshape(wide.shape[1:])


def update_row(row, rows, wide, weights_out):
    width = wide.shape[1] // rows
    tiles = [wide[tile, pl.ds(row, width, stride=rows), :] for tile in range(wide.shape[0])]
    return project(scale_rows(jnp.concatenate(tiles, axis=1)), weights_out)


def open_row(row, place, chain_each, chain_all, embed, pair_act):
    same_embed, other_embed = (
        jnp.broadcast_to(embed[step : step + 1, :], (8, embed.shape[1])).T[:, 0:1]
        for step in range(2)
    )
    same = chain_all[...] == chain_each[place]
    return pair_act[row].astype(jnp.float32).T + jnp.where(same, same_embed, other_embed)


def open_kernel(
    first, crop_each, chain_each, crop_all, chain_all, embed, weights_in, pair_act, parts, staged
):
    rows = pair_act.shape[0]
    width = staged.shape[2] // rows
    weights = turn(weights_in[0][:, : 4 * width])
    crop = crop_all[...].astype(jnp.float32)
    for row in range(rows):
        place = first[0] + row
        channels = open_row(row, place, chain_each, chain_all, embed, pair_act)
        mask = crop * crop_each[place].astype(jnp.float32)
        stage_row(row, rows, channels, weights, mask, staged)
    collect(staged, parts)


def gate_of(channels, weights):
    return jax.nn.sigmoid(project(scale_rows(channels), weights))


def open_gate_kernel(first, chain_each, chain_all, embed, weights_in, pair_act, pair_sum, gate):
    weights = turn(weights_in[0][:, weights_in.shape[2] - pair_sum.shape[1] :])
    for row in range(pair_act.shape[0]):
        channels = open_row(row, first[0] + row, chain_each, chain_all, embed, pair_act)
        pair_sum[row] = channels
        gate[row] = gate_of(channels, weights)


def start_copies(source, target, sems, row):
    copies = [
        pltpu.make_async_copy(one.at[row], other.at[row], sems.at[side, row])
        for side, (one, other) in enumerate(zip(source, target))
    ]
    for copy in copies:
        copy.start()
    return copies


def middle_kernel(
    first,
    crop_each,
    crop_all,
    weights_out,
    weights_in,
    products,
    pair_from,
    gate_from,
    parts,
    pair_far,
    wide,
    staged,
    pair_sum,
    gate,
    pair_next,
    sems,
    next_sems,
):
    rows = pair_sum.shape[0]
    width = staged.shape[2] // rows
    arriving = [
        start_copies((pair_from, gate_from), (pair_sum, gate), sems, row) for row in range(rows)
    ]
    widen(products, wide)
    weights, turned = turn(weights_in[1][:, : 4 * width]), turn(weights_out[0])
    crop = crop_all[...].astype(jnp.float32)
    leaving = []
    for row in range(rows):
        mask = crop * crop_each[first[0] + row].astype(jnp.float32)
        update = update_row(row, rows, wide, turned)
        for copy in arriving[row]:
            copy.wait()
        channels = pair_sum[row] + gate[row] * update
        pair_next[row] = channels
        leaving += start_copies((pair_next,), (pair_far,), next_sems, row)
        stage_row(row, rows, channels, weights, mask, staged)
    collect(staged, parts)
    for copy in leaving:
        copy.wait()


def middle_gate_kernel(weights_in, pair_sum, gate):
    weights = turn(weights_in[1][:, weights_in.shape[2] - pair_sum.shape[1] :])
    for row in range(pair_sum.shape[0]):
        gate[row] = gate_of(pair_sum[row], weights)


def close_kernel(
    weights_out, products, pair_from, gate_from, pair_new, wide, pair_sum, gate, sems
):
    rows = pair_sum.shape[0]
    arriving = [
        start_copies((pair_from, gate_from), (pair_sum, gate), sems, row) for row in range(rows)
    ]
    widen(products, wide)
    turned = turn(weights_out[1])
    for row in range(rows):
        update = update_row(row, rows, wide, turned)
        for copy in arriving[row]:
            copy.wait()
        pair_new[row] = (pair_sum[row] + gate[row] * update).T.astype(pair_new.dtype)


def attend_kernel(key_bias, score_proj, value_gate, column_out, got, out, wide, staged):
    tiles, held, _ = wide.shape
    seqs = key_bias.shape[0]
    rows = held // seqs
    for tile in range(tiles):
        piece = got[:, :, tile * LANES : (tile + 1) * LANES]
        wide[tile] = piece.astype(jnp.float32).reshape(held, LANES)
    query, value, gates, last = (
        turn(weights) for weights in (score_proj[0], value_gate[0], value_gate[1], column_out[...])
    )
    bias = jnp.broadcast_to(key_bias[...], (seqs, seqs))

    def attend(row, carry):
        column = jnp.concatenate(
            [wide[tile, pl.ds(row, seqs, stride=rows), :] for tile in range(tiles)], axis=1
        )
        normed_wide = normalize(column, 1)
        normed = normed_wide.astype(jnp.bfloat16)
        turned = normed_wide.T.astype(jnp.bfloat16)
        queries = (project(turned, query) * HEAD_DIM ** (-0.5)).astype(jnp.bfloat16)
        key_rows = project(score_proj[1], normed).astype(jnp.bfloat16)
        value_rows = project(turned, value).astype(jnp.bfloat16)
        gate_rows = jax.nn.sigmoid(project(turned, gates))
        mixture = []
        for head in range(HEADS):
            span = slice(head * HEAD_DIM, (head + 1) * HEAD_DIM)
            scores = project(queries[span], key_rows[:, span]) + bias
            raised = jnp.exp(scores - jnp.max(scores, axis=0, keepdims=True))
            weights = raised * (1.0 / jnp.sum(raised, axis=0, keepdims=True))
            mixture.append(project(weights.astype(jnp.bfloat16), value_rows[span]))
        gated = (gate_rows * jnp.concatenate(mixture, axis=0)).astype(jnp.bfloat16)
        column += project(gated, last).T
        for tile in range(tiles):
            staged[tile, pl.ds(row, seqs, stride=rows), :] = column[
                :, tile * LANES : (tile + 1) * LANES
            ]
        return carry

    lax.fori_loop(0, rows, attend, 0)
    for tile in range(tiles):
        out[:, tile * LANES : (tile + 1) * LANES] = staged[tile].astype(out.dtype)


KERNEL = pltpu.CompilerParams(vmem_limit_bytes=60 * 1024 * 1024)
HERE = pl.BlockSpec(memory_space=pltpu.VMEM)
EACH = pl.BlockSpec(memory_space=pltpu.SMEM)
FAR = pl.BlockSpec(memory_space=pl.ANY)


def shapes_of(rows, side, channels, devices):
    parts = jax.ShapeDtypeStruct((devices, 2 * channels * rows // devices, side), jnp.bfloat16)
    held = jax.ShapeDtypeStruct((rows, channels, side), jnp.float32)
    tiles = (side // LANES, channels * rows, LANES)
    return (
        parts,
        held,
        pltpu.VMEM(tiles, jnp.float32),
        pltpu.VMEM((2,) + tiles, jnp.float32),
    )


def open_pair(first, crop, chains, embed, weights_in, pair_act, devices):
    parts, _, _, staged = shapes_of(*pair_act.shape, devices)
    return pl.pallas_call(
        open_kernel,
        in_specs=[EACH] * 3 + [HERE] * 5,
        out_specs=HERE,
        out_shape=parts,
        scratch_shapes=[staged],
        compiler_params=KERNEL,
    )(first, crop, chains, crop[None], chains[None], embed, weights_in, pair_act)


def open_gate(first, chains, embed, weights_in, pair_act, devices):
    _, held, _, _ = shapes_of(*pair_act.shape, devices)
    return pl.pallas_call(
        open_gate_kernel,
        in_specs=[EACH] * 2 + [HERE] * 4,
        out_specs=(HERE, HERE),
        out_shape=(held, held),
        compiler_params=KERNEL,
    )(first, chains, chains[None], embed, weights_in, pair_act)


def middle_pair(first, crop, weights_out, weights_in, products, pair_sum, gate):
    rows, channels, side = pair_sum.shape
    devices, held, lanes = products.shape
    parts, pair_next, wide, staged = shapes_of(rows, side, channels, devices)
    near = pltpu.VMEM(pair_sum.shape, jnp.float32)
    return pl.pallas_call(
        middle_kernel,
        grid=(1,),
        in_specs=[EACH] * 2
        + [HERE] * 3
        + [pl.BlockSpec((devices, held // 2, lanes), lambda step: (0, 0, 0)), FAR, FAR],
        out_specs=(HERE, FAR),
        out_shape=(parts, pair_next),
        scratch_shapes=[wide, staged, near, near, near]
        + [pltpu.SemaphoreType.DMA((2, rows)), pltpu.SemaphoreType.DMA((1, rows))],
        compiler_params=KERNEL,
    )(first, crop, crop[None], weights_out, weights_in, products, pair_sum, gate)


def middle_gate(weights_in, pair_sum):
    return pl.pallas_call(
        middle_gate_kernel,
        in_specs=[HERE] * 2,
        out_specs=HERE,
        out_shape=jax.ShapeDtypeStruct(pair_sum.shape, jnp.float32),
        compiler_params=KERNEL,
    )(weights_in, pair_sum)


def close_pair(weights_out, products, pair_sum, gate):
    rows, channels, side = pair_sum.shape
    _, _, wide, _ = shapes_of(rows, side, channels, products.shape[0])
    near = pltpu.VMEM(pair_sum.shape, jnp.float32)
    return pl.pallas_call(
        close_kernel,
        in_specs=[HERE] * 2 + [FAR] * 2,
        out_specs=HERE,
        out_shape=jax.ShapeDtypeStruct((rows, side, channels), jnp.bfloat16),
        scratch_shapes=[wide, near, near, pltpu.SemaphoreType.DMA((2, rows))],
        compiler_params=KERNEL,
    )(weights_out, products, pair_sum, gate)


def attend_columns(key_bias, score_proj, value_gate, column_out, got, rows):
    devices, held, depth = got.shape
    seqs = key_bias.shape[0]
    wide = pltpu.VMEM((depth // LANES, seqs * rows, LANES), jnp.float32)
    moves = seqs * depth * (4 * depth + 2 * seqs + depth)
    return pl.pallas_call(
        attend_kernel,
        grid=(1,),
        in_specs=[HERE] * 4 + [pl.BlockSpec((devices, held // 2, depth), lambda step: (0, 1, 0))],
        out_specs=HERE,
        out_shape=jax.ShapeDtypeStruct((seqs * rows, depth), jnp.bfloat16),
        scratch_shapes=[wide, wide],
        compiler_params=KERNEL,
        cost_estimate=pl.CostEstimate(
            flops=2 * rows * moves,
            bytes_accessed=4 * seqs * rows * depth,
            transcendentals=rows * seqs * (HEADS * seqs + depth),
        ),
    )(key_bias[:, None], score_proj, value_gate, column_out, got)


def split_parts(both, share, rows):
    devices, held, side = both.shape
    both = both.reshape(devices, 2, share, rows, side)
    return both[:, 0], both[:, 1]


def block_products(products, devices, lanes):
    share, side, _ = products.shape
    blocks = products.reshape(share, devices, side // devices, side // lanes, lanes)
    return blocks.transpose(1, 3, 0, 2, 4).reshape(devices, -1, lanes)


def exchange_blocks(blocks):
    return lax.all_to_all(blocks, "dap", split_axis=0, concat_axis=0, tiled=True)


def on_device(
    alignment,
    pair_act,
    crop_mask,
    seq_mask,
    chain_ids,
    chain_embed,
    score_proj,
    value_gate,
    column_out,
    triangle_in,
    triangle_out,
):
    rows_here = pair_act.shape[0]
    width = triangle_out.shape[1]
    devices = lax.axis_size("dap")
    row_start = lax.axis_index("dap") * rows_here
    share = width // devices
    seq_here, _, depth = alignment.shape
    sent = alignment.reshape(seq_here, devices, rows_here, depth)
    sent = jnp.moveaxis(sent, 1, 0).reshape(devices, -1, depth)
    carrier = jnp.concatenate([jnp.zeros_like(sent), sent], axis=1)

    kept_rows = jnp.maximum(seq_mask, (jnp.arange(seq_mask.shape[0]) == 0).astype(jnp.int32))
    key_bias = (kept_rows - 1).astype(jnp.float32) * 1000000000.0
    first_row = row_start.reshape(1).astype(jnp.int32)
    parts = open_pair(
        first_row, crop_mask, chain_ids, chain_embed, triangle_in, pair_act, devices
    )
    both = exchange_blocks(parts)
    pair_sum, gate = open_gate(first_row, chain_ids, chain_embed, triangle_in, pair_act, devices)
    both, carrier, pair_sum, gate = lax.optimization_barrier((both, carrier, pair_sum, gate))
    left, right = split_parts(both, share, rows_here)
    left = jnp.moveaxis(left, 1, 0).reshape(share, -1, left.shape[-1])
    right = jnp.moveaxis(right, 1, 0).reshape(share, -1, right.shape[-1])
    products = jnp.einsum(
        "cik,cjk->cij", left, right, preferred_element_type=jnp.float32
    ).astype(jnp.bfloat16)
    products = block_products(products, devices, depth)
    got = exchange_blocks(lax.dynamic_update_slice(carrier, products, (0, 0, 0)))
    parts, pair_sum = middle_pair(
        first_row, crop_mask, triangle_out, triangle_in, got, pair_sum, gate
    )
    parts, got = lax.optimization_barrier((parts, got))
    both = exchange_blocks(parts)
    attended = attend_columns(key_bias, score_proj, value_gate, column_out, got, rows_here)
    both, attended, pair_sum = lax.optimization_barrier((both, attended, pair_sum))
    left, right = split_parts(both, share, rows_here)
    left = jnp.moveaxis(left, 1, 0).reshape(share, -1, left.shape[-1])
    right = jnp.moveaxis(right, 1, 0).reshape(share, -1, right.shape[-1])
    products = jnp.einsum(
        "cki,ckj->cij", left, right, preferred_element_type=jnp.float32
    ).astype(jnp.bfloat16)
    products = exchange_blocks(block_products(products, devices, products.shape[-1]))
    gate = middle_gate(triangle_in, pair_sum)
    alignment_new = attended.reshape(-1, rows_here, depth)
    products, gate = lax.optimization_barrier((products, gate))
    pair_new = close_pair(triangle_out, products, pair_sum, gate)
    return (alignment_new, pair_new)


def solution(mesh):
    placed = (
        P(("dp", "dap"), None, None),
        P(("dp", "dap"), None, None),
        P("dp"),
        P("dp"),
        P("dp"),
        P(),
        P(),
        P(),
        P(),
        P(),
        P(),
    )
    return jax.shard_map(
        on_device,
        mesh=mesh,
        in_specs=placed,
        out_specs=(P("dp", "dap", None), P(("dp", "dap"), None, None)),
        check_vma=False,
    )
```

time: 509 us -> 408 us (0.80)
  matrix products: 90.6 us -> 1.5 us
  Pallas kernels: 0 us -> 57.8 us
  blocking collectives: 59.1 us -> 104 us
  waiting for transfers between devices: 240 us -> 202 us
  local copies, waits for them, and re-layouts: 34.8 us -> 6.64 us
  other arithmetic: 23.7 us -> 0.01 us
  starting transfers between devices: 56.9 us -> 34.5 us
    dot_general x48 -> x2, matrix products: 84.4 us -> 1.5 us  [the longest x1 0.76 us: on_device(): jnp.einsum('cki,ckj->cij', left, right, preferred_element_type=jnp.float32)]
    pallas_call x0 -> x6, Pallas kernels: none -> 57.8 us  [the longest x1 29.7 us: attend_columns(): pl.pallas_call(attend_kernel, grid=(1,), in_specs=[HERE] * 4 + [pl.BlockS...]
    all_to_all x1, blocking collectives: 59.1 us -> 104 us  [exchange_blocks(): lax.all_to_all(blocks, 'dap', split_axis=0, concat_axis=0, tiled=True)]
    all_to_all x6 -> x3, waiting for transfers between devices: 240 us -> 202 us  [exchange_blocks(): lax.all_to_all(blocks, 'dap', split_axis=0, concat_axis=0, tiled=True)]
    all_to_all x6 -> x3, starting transfers between devices: 56.9 us -> 34.5 us  [exchange_blocks(): lax.all_to_all(blocks, 'dap', split_axis=0, concat_axis=0, tiled=True)]
    reduce_sum x23 -> x0, other arithmetic: 19 us -> none  [the longest x12 10.2 us: normalize(): variance = jnp.mean(centered * centered, axis=axis, keepdims=True)]
    convert_element_type x8 -> x0, local copies, waits for them, and re-layouts: 14.6 us -> none  [the longest x2 4.36 us: project_pair(): right_part = (jax.nn.sigmoid(projected[:, 2 * width:3 * width]) * project...]
    sub x8 -> x0, matrix products: 6.15 us -> none  [column_update(): raised = jnp.exp(scores - highest)]
  transfers between devices with their start and end apart: 6 -> 3, of which waited for: 5 -> 3; matrix products, arithmetic and copies ran while one was open for 24% -> 1% of each run, Pallas kernels for 0% -> 9%
where the time goes in v3:
time: 408 us; the launch traced here: 407 us
  waiting for transfers between devices  202 us (50%)
  blocking collectives  104 us (25%)
  Pallas kernels  57.8 us (14%)
  starting transfers between devices  34.5 us (8%)
  local copies, waits for them, and re-layouts  6.64 us (2%)
    all_to_all x3, waiting for transfers between devices, exchange_blocks(): lax.all_to_all(blocks, 'dap', split_axis=0, concat_axis=0, tiled=True)  202 us
    all_to_all x1, blocking collectives, exchange_blocks(): lax.all_to_all(blocks, 'dap', split_axis=0, concat_axis=0, tiled=True)  104 us
    all_to_all x3, starting transfers between devices, exchange_blocks(): lax.all_to_all(blocks, 'dap', split_axis=0, concat_axis=0, tiled=True)  34.5 us
    pallas_call x1, Pallas kernels, attend_columns(): pl.pallas_call(attend_kernel, grid=(1,), in_specs=[HERE] * 4 + [pl.BlockS...  29.7 us
    pallas_call x1, Pallas kernels, middle_pair(): pl.pallas_call(middle_kernel, grid=(1,), in_specs=[EACH] * 2 + [HERE] * 3...  8.21 us
  transfers between devices with their start and end apart: 3, of which 3 were waited for; matrix products, arithmetic and copies ran while one was open for 1% of the time, Pallas kernels for 9%

profile of v3, /device:TPU:1, one launch (start us, length us, event | category | flops | bytes accessed | tf_op | source)
XLA Modules:
  0.0 407.1 jit_solution(2809159743452248813)
XLA Ops:
  0.6 0.0 copy-start
  0.6 5.6 %shard_map.122 = bf16[64,32,512]{2,1,0:T(8,128)(2,1)} custom-call(s32[1]{0:T(128)} %bitcast.first, s32[512]{0:T(512)} %crop_each.3, s32[512]{0:T(512)} %chain_each.3, s32[1,512]{1,0:T(1,128)} %bitcast.59, s32[1,512]{1,0:T(1,128)} %bitcast.57, f32[2,128]{1,0:T(2,128)} %embed.3, bf16[2,128,640]{2,1,0:T(8,128)(2,1)} %weights_in.7, bf16[8,512,128]{2,1,0:T(8,128)(2,1)} %pair_act.3), custom_call_target="tpu_custom_call" | custom-call | tf_op jit(solution)/shard_map/pallas_call | solution.py:253
  6.3 17.2 %all-to-all-start = ((bf16[64,32,512]{2,1,0:T(8,128)(2,1)}), bf16[64,32,512]{2,1,0:T(8,128)(2,1)S(1)}, u32[]{:S(2)}, u32[]{:S(2)}) async-start(bf16[64,32,512]{2,1,0:T(8,128)(2,1)} %shard_map.122), calls=%async_computation | async-start | bytes 4194304 | tf_op jit(solution)/shard_map/all_to_all | solution.py:351
  23.5 4.8 %shard_map.123 = (f32[8,128,512]{2,1,0:T(8,128)}, f32[8,128,512]{2,1,0:T(8,128)}) custom-call(s32[1]{0:T(128)} %bitcast.first, s32[512]{0:T(512)} %chain_each.3, s32[1,512]{1,0:T(1,128)} %bitcast.58, f32[2,128]{1,0:T(2,128)} %embed.3, bf16[2,128,640]{2,1,0:T(8,128)(2,1)} %weights_in.7, bf16[8,512,128]{2,1,0:T(8,128)(2,1)} %pair_act.3), custom_call_target="tpu_custom_call" | custom-call | tf_op jit(solution)/shard_map/pallas_call | solution.py:265
  28.3 0.0 copy-done
  28.3 0.1 copy_bitcast_fusion.3
  28.5 1.6 concatenate.3
  30.1 89.0 %all-to-all-done = bf16[64,32,512]{2,1,0:T(8,128)(2,1)S(1)} async-done(((bf16[64,32,512]{2,1,0:T(8,128)(2,1)}), bf16[64,32,512]{2,1,0:T(8,128)(2,1)S(1)}, u32[]{:S(2)}, u32[]{:S(2)}) %all-to-all-start) | async-done | bytes 2097184 | tf_op jit(solution)/shard_map/all_to_all | solution.py:351
  119.1 0.2 slice_bitcast_fusion.2
  119.3 0.7 convolution_convert_fusion.1
  120.0 0.0 copy-start.1
  120.0 0.1 copy.23
  120.2 1.4 copy-done.1
  121.6 0.1 constant_dynamic-update-slice_fusion
  121.7 104.1 %all_to_all.20.products.got = bf16[64,64,256]{2,1,0:T(8,128)(2,1)} all-to-all(bf16[64,64,256]{2,1,0:T(8,128)(2,1)S(1)} %constant_dynamic-update-slice_fusion), channel_id=1, replica_groups=mesh['dp'=8,'dap'=64] {'dap'}, dimensions={0} | all-to-all | bytes 4194304 | tf_op jit(solution)/shard_map/all_to_all | solution.py:351
  225.8 8.2 %shard_map.124 = (bf16[64,32,512]{2,1,0:T(8,128)(2,1)}, f32[8,128,512]{2,1,0:T(8,128)}) custom-call(s32[1]{0:T(128)} %bitcast.first, s32[512]{0:T(512)} %crop_each.3, s32[1,512]{1,0:T(1,128)} %bitcast.60, bf16[2,128,128]{2,1,0:T(8,128)(2,1)} %weights_out.3, bf16[2,128,640]{2,1,0:T(8,128)(2,1)} %weights_in.7, bf16[64,64,256]{2,1,0:T(8,128)(2,1)} %all_to_all.20.products.got, ...), custom_call_target="tpu_custom_call" | custom-call | tf_op jit(solution)/shard_map/pallas_call | solution.py:279
  234.0 0.0 copy-start.3
  234.1 8.7 %all-to-all-start.2 = ((bf16[64,32,512]{2,1,0:T(8,128)(2,1)}), bf16[64,32,512]{2,1,0:T(8,128)(2,1)S(1)}, u32[]{:S(2)}, u32[]{:S(2)}) async-start(bf16[64,32,512]{2,1,0:T(8,128)(2,1)} %get-tuple-element.24), calls=%async_computation.2 | async-start | bytes 4194304 | tf_op jit(solution)/shard_map/all_to_all | solution.py:351
  242.7 0.0 copy-done.3
  242.7 0.8 copy.24.key_bias
  243.5 29.7 %shard_map.125 = bf16[2048,256]{1,0:T(8,128)(2,1)} custom-call(f32[256,1]{1,0:T(8,128)} %copy.24.key_bias, bf16[2,256,256]{2,1,0:T(8,128)(2,1)} %score_proj.1, bf16[2,256,256]{2,1,0:T(8,128)(2,1)} %value_gate.1, bf16[256,256]{1,0:T(8,128)(2,1)} %column_out.1, bf16[64,64,256]{2,1,0:T(8,128)(2,1)} %all_to_all.20.products.got), custom_call_target="tpu_custom_call" | custom-call | flops 1879048192 | bytes 2097152 | tf_op jit(solution)/shard_map/pallas_call | solution.py:322
  273.2 65.1 %all-to-all-done.2 = bf16[64,32,512]{2,1,0:T(8,128)(2,1)S(1)} async-done(((bf16[64,32,512]{2,1,0:T(8,128)(2,1)}), bf16[64,32,512]{2,1,0:T(8,128)(2,1)S(1)}, u32[]{:S(2)}, u32[]{:S(2)}) %all-to-all-start.2) | async-done | bytes 2097184 | tf_op jit(solution)/shard_map/all_to_all | solution.py:351
  338.3 0.2 slice_bitcast_fusion
  338.5 0.8 fusion
  339.3 1.1 copy.47
  340.4 8.6 %all-to-all-start.3 = ((bf16[64,16,512]{2,1,0:T(8,128)(2,1)}), bf16[64,16,512]{2,1,0:T(8,128)(2,1)S(1)}, u32[]{:S(2)}, u32[]{:S(2)}) async-start(bf16[64,16,512]{2,1,0:T(8,128)(2,1)} %bitcast.52), calls=%async_computation.3 | async-start | bytes 2097152 | tf_op jit(solution)/shard_map/all_to_all | solution.py:351
  349.0 3.9 shard_map.126.gate_from
  352.9 47.6 %all-to-all-done.3.products = bf16[64,16,512]{2,1,0:T(8,128)(2,1)S(1)} async-done(((bf16[64,16,512]{2,1,0:T(8,128)(2,1)}), bf16[64,16,512]{2,1,0:T(8,128)(2,1)S(1)}, u32[]{:S(2)}, u32[]{:S(2)}) %all-to-all-start.3) | async-done | bytes 1048608 | tf_op jit(solution)/shard_map/all_to_all | solution.py:351
  400.5 0.0 copy-start.2
  400.5 1.0 copy-done.2
  401.4 5.5 %shard_map.127 = bf16[8,512,128]{2,1,0:T(8,128)(2,1)} custom-call(bf16[2,128,128]{2,1,0:T(8,128)(2,1)} %weights_out.3, bf16[64,16,512]{2,1,0:T(8,128)(2,1)} %copy-done.2, f32[8,128,512]{2,1,0:T(8,128)} %get-tuple-element.29.pair_sum.pair_from, f32[8,128,512]{2,1,0:T(8,128)} %shard_map.126.gate_from), custom_call_target="tpu_custom_call" | custom-call | tf_op jit(solution)/shard_map/pallas_call | solution.py:307
  (1 shorter events, 0.0 us)
Async XLA Ops:
  0.6 27.7 %copy-start = (bf16[4,512,256]{2,1,0:T(8,128)(2,1)S(1)}, bf16[4,512,256]{2,1,0:T(8,128)(2,1)}, u32[]{:S(2)}) copy-start(bf16[4,512,256]{2,1,0:T(8,128)(2,1)} %param.11) | copy-start | bytes 3145732
  6.3 112.8 %all-to-all-start = ((bf16[64,32,512]{2,1,0:T(8,128)(2,1)}), bf16[64,32,512]{2,1,0:T(8,128)(2,1)S(1)}, u32[]{:S(2)}, u32[]{:S(2)}) async-start(bf16[64,32,512]{2,1,0:T(8,128)(2,1)} %shard_map.122), calls=%async_computation | async-start | bytes 4194304 | tf_op jit(solution)/shard_map/all_to_all | solution.py:351
  120.0 1.6 copy-start.1
  234.0 8.7 %copy-start.3 = (s32[256]{0:T(256)S(1)}, s32[256]{0:T(256)}, u32[]{:S(2)}) copy-start(s32[256]{0:T(256)} %param.14) | copy-start | bytes 3076
  234.1 104.2 %all-to-all-start.2 = ((bf16[64,32,512]{2,1,0:T(8,128)(2,1)}), bf16[64,32,512]{2,1,0:T(8,128)(2,1)S(1)}, u32[]{:S(2)}, u32[]{:S(2)}) async-start(bf16[64,32,512]{2,1,0:T(8,128)(2,1)} %get-tuple-element.24), calls=%async_computation.2 | async-start | bytes 4194304 | tf_op jit(solution)/shard_map/all_to_all | solution.py:351
  340.4 60.1 %all-to-all-start.3 = ((bf16[64,16,512]{2,1,0:T(8,128)(2,1)}), bf16[64,16,512]{2,1,0:T(8,128)(2,1)S(1)}, u32[]{:S(2)}, u32[]{:S(2)}) async-start(bf16[64,16,512]{2,1,0:T(8,128)(2,1)} %bitcast.52), calls=%async_computation.3 | async-start | bytes 2097152 | tf_op jit(solution)/shard_map/all_to_all | solution.py:351
  400.5 1.0 copy-start.2

commit v4 on v3

--- a/solution.py
+++ b/solution.py
@@ -105,12 +105,11 @@
     return jax.nn.sigmoid(project(scale_rows(channels), weights))
 
 
-def open_gate_kernel(first, chain_each, chain_all, embed, weights_in, pair_act, pair_sum, gate):
-    weights = turn(weights_in[0][:, weights_in.shape[2] - pair_sum.shape[1] :])
+def open_gate_kernel(first, chain_each, chain_all, embed, weights_in, pair_act, gate):
+    weights = turn(weights_in[0][:, weights_in.shape[2] - gate.shape[1] :])
     for row in range(pair_act.shape[0]):
         channels = open_row(row, first[0] + row, chain_each, chain_all, embed, pair_act)
-        pair_sum[row] = channels
-        gate[row] = gate_of(channels, weights)
+        gate[row] = gate_of(channels, weights).astype(gate.dtype)
 
 
 def start_copies(source, target, sems, row):
@@ -126,53 +125,72 @@
 def middle_kernel(
     first,
     crop_each,
+    chain_each,
     crop_all,
+    chain_all,
+    embed,
     weights_out,
     weights_in,
     products,
     pair_from,
     gate_from,
     parts,
-    pair_far,
     wide,
     staged,
-    pair_sum,
+    pair_act,
     gate,
-    pair_next,
+    updates,
     sems,
-    next_sems,
 ):
-    rows = pair_sum.shape[0]
+    rows = pair_act.shape[0]
     width = staged.shape[2] // rows
     arriving = [
-        start_copies((pair_from, gate_from), (pair_sum, gate), sems, row) for row in range(rows)
+        start_copies((pair_from, gate_from), (pair_act, gate), sems, row) for row in range(rows)
     ]
     widen(products, wide)
     weights, turned = turn(weights_in[1][:, : 4 * width]), turn(weights_out[0])
     crop = crop_all[...].astype(jnp.float32)
-    leaving = []
-    for row in range(rows):
-        mask = crop * crop_each[first[0] + row].astype(jnp.float32)
-        update = update_row(row, rows, wide, turned)
-        for copy in arriving[row]:
+    for row in range(rows):
+        updates[row] = update_row(row, rows, wide, turned)
+    for copies in arriving:
+        for copy in copies:
             copy.wait()
-        channels = pair_sum[row] + gate[row] * update
-        pair_next[row] = channels
-        leaving += start_copies((pair_next,), (pair_far,), next_sems, row)
+    for row in range(rows):
+        place = first[0] + row
+        mask = crop * crop_each[place].astype(jnp.float32)
+        channels = open_row(row, place, chain_each, chain_all, embed, pair_act)
+        channels += gate[row].astype(jnp.float32) * updates[row]
         stage_row(row, rows, channels, weights, mask, staged)
     collect(staged, parts)
-    for copy in leaving:
-        copy.wait()
-
-
-def middle_gate_kernel(weights_in, pair_sum, gate):
-    weights = turn(weights_in[1][:, weights_in.shape[2] - pair_sum.shape[1] :])
-    for row in range(pair_sum.shape[0]):
-        gate[row] = gate_of(pair_sum[row], weights)
+
+
+def middle_gate_kernel(
+    first,
+    chain_each,
+    chain_all,
+    embed,
+    weights_out,
+    weights_in,
+    products,
+    pair_act,
+    gate,
+    pair_next,
+    gate_next,
+    wide,
+):
+    rows = pair_act.shape[0]
+    weights = turn(weights_in[1][:, weights_in.shape[2] - gate.shape[1] :])
+    widen(products, wide)
+    turned = turn(weights_out[0])
+    for row in range(rows):
+        channels = open_row(row, first[0] + row, chain_each, chain_all, embed, pair_act)
+        channels += gate[row].astype(jnp.float32) * update_row(row, rows, wide, turned)
+        pair_next[row] = channels
+        gate_next[row] = gate_of(channels, weights).astype(gate_next.dtype)
 
 
 def close_kernel(
-    weights_out, products, pair_from, gate_from, pair_new, wide, pair_sum, gate, sems
+    weights_out, products, pair_from, gate_from, pair_new, wide, pair_sum, gate, updates, sems
 ):
     rows = pair_sum.shape[0]
     arriving = [
@@ -181,10 +199,13 @@
     widen(products, wide)
     turned = turn(weights_out[1])
     for row in range(rows):
-        update = update_row(row, rows, wide, turned)
-        for copy in arriving[row]:
+        updates[row] = update_row(row, rows, wide, turned)
+    for copies in arriving:
+        for copy in copies:
             copy.wait()
-        pair_new[row] = (pair_sum[row] + gate[row] * update).T.astype(pair_new.dtype)
+    for row in range(rows):
+        channels = pair_sum[row] + gate[row].astype(jnp.float32) * updates[row]
+        pair_new[row] = channels.T.astype(pair_new.dtype)
 
 
 def attend_kernel(key_bias, score_proj, value_gate, column_out, got, out, wide, staged):
@@ -260,44 +281,66 @@
     )(first, crop, chains, crop[None], chains[None], embed, weights_in, pair_act)
 
 
-def open_gate(first, chains, embed, weights_in, pair_act, devices):
-    _, held, _, _ = shapes_of(*pair_act.shape, devices)
+def open_gate(first, chains, embed, weights_in, pair_act):
+    rows, side, channels = pair_act.shape
     return pl.pallas_call(
         open_gate_kernel,
         in_specs=[EACH] * 2 + [HERE] * 4,
-        out_specs=(HERE, HERE),
-        out_shape=(held, held),
+        out_specs=HERE,
+        out_shape=jax.ShapeDtypeStruct((rows, channels, side), jnp.bfloat16),
         compiler_params=KERNEL,
     )(first, chains, chains[None], embed, weights_in, pair_act)
 
 
-def middle_pair(first, crop, weights_out, weights_in, products, pair_sum, gate):
-    rows, channels, side = pair_sum.shape
-    devices, held, lanes = products.shape
-    parts, pair_next, wide, staged = shapes_of(rows, side, channels, devices)
-    near = pltpu.VMEM(pair_sum.shape, jnp.float32)
+def first_half(blocks):
+    devices, held, lanes = blocks.shape
+    return pl.BlockSpec((devices, held // 2, lanes), lambda step: (0, 0, 0))
+
+
+def middle_pair(first, crop, chains, embed, weights_out, weights_in, products, pair_act, gate):
+    parts, held, wide, staged = shapes_of(*pair_act.shape, products.shape[0])
+    rows = pair_act.shape[0]
     return pl.pallas_call(
         middle_kernel,
         grid=(1,),
-        in_specs=[EACH] * 2
-        + [HERE] * 3
-        + [pl.BlockSpec((devices, held // 2, lanes), lambda step: (0, 0, 0)), FAR, FAR],
-        out_specs=(HERE, FAR),
-        out_shape=(parts, pair_next),
-        scratch_shapes=[wide, staged, near, near, near]
-        + [pltpu.SemaphoreType.DMA((2, rows)), pltpu.SemaphoreType.DMA((1, rows))],
-        compiler_params=KERNEL,
-    )(first, crop, crop[None], weights_out, weights_in, products, pair_sum, gate)
-
-
-def middle_gate(weights_in, pair_sum):
+        in_specs=[EACH] * 3 + [HERE] * 5 + [first_half(products), FAR, FAR],
+        out_specs=HERE,
+        out_shape=parts,
+        scratch_shapes=[
+            wide,
+            staged,
+            pltpu.VMEM(pair_act.shape, pair_act.dtype),
+            pltpu.VMEM(gate.shape, gate.dtype),
+            pltpu.VMEM(held.shape, held.dtype),
+            pltpu.SemaphoreType.DMA((2, rows)),
+        ],
+        compiler_params=KERNEL,
+    )(
+        first,
+        crop,
+        chains,
+        crop[None],
+        chains[None],
+        embed,
+        weights_out,
+        weights_in,
+        products,
+        pair_act,
+        gate,
+    )
+
+
+def middle_gate(first, chains, embed, weights_out, weights_in, products, pair_act, gate):
+    _, held, wide, _ = shapes_of(*pair_act.shape, products.shape[0])
     return pl.pallas_call(
         middle_gate_kernel,
-        in_specs=[HERE] * 2,
-        out_specs=HERE,
-        out_shape=jax.ShapeDtypeStruct(pair_sum.shape, jnp.float32),
-        compiler_params=KERNEL,
-    )(weights_in, pair_sum)
+        grid=(1,),
+        in_specs=[EACH] * 2 + [HERE] * 4 + [first_half(products), HERE, HERE],
+        out_specs=(HERE, HERE),
+        out_shape=(held, jax.ShapeDtypeStruct(gate.shape, gate.dtype)),
+        scratch_shapes=[wide],
+        compiler_params=KERNEL,
+    )(first, chains, chains[None], embed, weights_out, weights_in, products, pair_act, gate)
 
 
 def close_pair(weights_out, products, pair_sum, gate):
@@ -309,7 +352,13 @@
         in_specs=[HERE] * 2 + [FAR] * 2,
         out_specs=HERE,
         out_shape=jax.ShapeDtypeStruct((rows, side, channels), jnp.bfloat16),
-        scratch_shapes=[wide, near, near, pltpu.SemaphoreType.DMA((2, rows))],
+        scratch_shapes=[
+            wide,
+            near,
+            pltpu.VMEM(gate.shape, gate.dtype),
+            near,
+            pltpu.SemaphoreType.DMA((2, rows)),
+        ],
         compiler_params=KERNEL,
     )(weights_out, products, pair_sum, gate)
 
@@ -381,8 +430,8 @@
         first_row, crop_mask, chain_ids, chain_embed, triangle_in, pair_act, devices
     )
     both = exchange_blocks(parts)
-    pair_sum, gate = open_gate(first_row, chain_ids, chain_embed, triangle_in, pair_act, devices)
-    both, carrier, pair_sum, gate = lax.optimization_barrier((both, carrier, pair_sum, gate))
+    gate = open_gate(first_row, chain_ids, chain_embed, triangle_in, pair_act)
+    both, carrier, gate = lax.optimization_barrier((both, carrier, gate))
     left, right = split_parts(both, share, rows_here)
     left = jnp.moveaxis(left, 1, 0).reshape(share, -1, left.shape[-1])
     right = jnp.moveaxis(right, 1, 0).reshape(share, -1, right.shape[-1])
@@ -391,13 +440,12 @@
     ).astype(jnp.bfloat16)
     products = block_products(products, devices, depth)
     got = exchange_blocks(lax.dynamic_update_slice(carrier, products, (0, 0, 0)))
-    parts, pair_sum = middle_pair(
-        first_row, crop_mask, triangle_out, triangle_in, got, pair_sum, gate
-    )
+    pair_in = (chain_embed, triangle_out, triangle_in)
+    parts = middle_pair(first_row, crop_mask, chain_ids, *pair_in, got, pair_act, gate)
     parts, got = lax.optimization_barrier((parts, got))
     both = exchange_blocks(parts)
     attended = attend_columns(key_bias, score_proj, value_gate, column_out, got, rows_here)
-    both, attended, pair_sum = lax.optimization_barrier((both, attended, pair_sum))
+    both, attended, got = lax.optimization_barrier((both, attended, got))
     left, right = split_parts(both, share, rows_here)
     left = jnp.moveaxis(left, 1, 0).reshape(share, -1, left.shape[-1])
     right = jnp.moveaxis(right, 1, 0).reshape(share, -1, right.shape[-1])
@@ -405,9 +453,9 @@
         "cki,ckj->cij", left, right, preferred_element_type=jnp.float32
     ).astype(jnp.bfloat16)
     products = exchange_blocks(block_products(products, devices, products.shape[-1]))
-    gate = middle_gate(triangle_in, pair_sum)
+    pair_sum, gate = middle_gate(first_row, chain_ids, *pair_in, got, pair_act, gate)
     alignment_new = attended.reshape(-1, rows_here, depth)
-    products, gate = lax.optimization_barrier((products, gate))
+    products, pair_sum, gate = lax.optimization_barrier((products, pair_sum, gate))
     pair_new = close_pair(triangle_out, products, pair_sum, gate)
     return (alignment_new, pair_new)
 

time: 408 us -> 407 us (level)
  transfers between devices with their start and end apart: 3 -> 3, of which waited for: 3 -> 3; matrix products, arithmetic and copies ran while one was open for 1% -> 0% of each run, Pallas kernels for 9% -> 10%
where the time goes in v4:
time: 407 us; the launch traced here: 406 us
  waiting for transfers between devices  201 us (49%)
  blocking collectives  104 us (26%)
  Pallas kernels  58.3 us (14%)
  starting transfers between devices  34.7 us (9%)
  local copies, waits for them, and re-layouts  5.41 us (1%)
    all_to_all x3, waiting for transfers between devices, exchange_blocks(): lax.all_to_all(blocks, 'dap', split_axis=0, concat_axis=0, tiled=True)  201 us
    all_to_all x1, blocking collectives, exchange_blocks(): lax.all_to_all(blocks, 'dap', split_axis=0, concat_axis=0, tiled=True)  104 us
    all_to_all x3, starting transfers between devices, exchange_blocks(): lax.all_to_all(blocks, 'dap', split_axis=0, concat_axis=0, tiled=True)  34.7 us
    pallas_call x1, Pallas kernels, attend_columns(): pl.pallas_call(attend_kernel, grid=(1,), in_specs=[HERE] * 4 + [pl.BlockS...  29.7 us
  transfers between devices with their start and end apart: 3, of which 3 were waited for; matrix products, arithmetic and copies ran while one was open for 0% of the time, Pallas kernels for 10%

profile of v4, /device:TPU:1, one launch (start us, length us, event | category | flops | bytes accessed | tf_op | source)
XLA Modules:
  0.0 405.9 jit_solution(3454849615642255907)
XLA Ops:
  0.6 0.0 copy-start
  0.6 5.6 %shard_map.122 = bf16[64,32,512]{2,1,0:T(8,128)(2,1)} custom-call(s32[1]{0:T(128)} %bitcast.first, s32[512]{0:T(512)} %crop_each.3, s32[512]{0:T(512)} %chain_each.7, s32[1,512]{1,0:T(1,128)} %bitcast.60, s32[1,512]{1,0:T(1,128)} %bitcast.56, f32[2,128]{1,0:T(2,128)} %embed.7, bf16[2,128,640]{2,1,0:T(8,128)(2,1)} %weights_in.7, bf16[8,512,128]{2,1,0:T(8,128)(2,1)} %pair_act.5), custom_call_target="tpu_custom_call" | custom-call | tf_op jit(solution)/shard_map/pallas_call | solution.py:274
  6.2 17.4 %all-to-all-start = ((bf16[64,32,512]{2,1,0:T(8,128)(2,1)}), bf16[64,32,512]{2,1,0:T(8,128)(2,1)}, u32[]{:S(2)}, u32[]{:S(2)}) async-start(bf16[64,32,512]{2,1,0:T(8,128)(2,1)} %shard_map.122), calls=%async_computation | async-start | bytes 4194304 | tf_op jit(solution)/shard_map/all_to_all | solution.py:400
  23.7 4.2 %shard_map.123.gate_from.gate = bf16[8,128,512]{2,1,0:T(8,128)(2,1)} custom-call(s32[1]{0:T(128)} %bitcast.first, s32[512]{0:T(512)} %chain_each.7, s32[1,512]{1,0:T(1,128)} %bitcast.57, f32[2,128]{1,0:T(2,128)} %embed.7, bf16[2,128,640]{2,1,0:T(8,128)(2,1)} %weights_in.7, bf16[8,512,128]{2,1,0:T(8,128)(2,1)} %pair_act.5), custom_call_target="tpu_custom_call" | custom-call | tf_op jit(solution)/shard_map/pallas_call | solution.py:286
  27.8 0.0 copy-done
  27.8 0.1 copy_bitcast_fusion.3
  27.9 0.2 concatenate.3
  28.2 91.0 %all-to-all-done = bf16[64,32,512]{2,1,0:T(8,128)(2,1)} async-done(((bf16[64,32,512]{2,1,0:T(8,128)(2,1)}), bf16[64,32,512]{2,1,0:T(8,128)(2,1)}, u32[]{:S(2)}, u32[]{:S(2)}) %all-to-all-start) | async-done | bytes 2097184 | tf_op jit(solution)/shard_map/all_to_all | solution.py:400
  119.2 1.7 slice_bitcast_fusion.2
  120.9 0.7 convolution_convert_fusion.1
  121.6 0.1 copy.23
  121.8 0.1 constant_dynamic-update-slice_fusion
  121.9 104.1 %all_to_all.20.products.got = bf16[64,64,256]{2,1,0:T(8,128)(2,1)} all-to-all(bf16[64,64,256]{2,1,0:T(8,128)(2,1)S(1)} %constant_dynamic-update-slice_fusion), channel_id=1, replica_groups=mesh['dp'=8,'dap'=64] {'dap'}, dimensions={0} | all-to-all | bytes 4194304 | tf_op jit(solution)/shard_map/all_to_all | solution.py:400
  226.0 7.7 %shard_map.124 = bf16[64,32,512]{2,1,0:T(8,128)(2,1)} custom-call(s32[1]{0:T(128)} %bitcast.first, s32[512]{0:T(512)} %crop_each.3, s32[512]{0:T(512)} %chain_each.7, s32[1,512]{1,0:T(1,128)} %bitcast.61, s32[1,512]{1,0:T(1,128)} %bitcast.58, f32[2,128]{1,0:T(2,128)} %embed.7, bf16[2,128,128]{2,1,0:T(8,128)(2,1)} %weights_out.5, ...), custom_call_target="tpu_custom_call" | custom-call | tf_op jit(solution)/shard_map/pallas_call | solution.py:303
  233.8 0.0 copy-start.2
  233.8 8.6 %all-to-all-start.2 = ((bf16[64,32,512]{2,1,0:T(8,128)(2,1)}), bf16[64,32,512]{2,1,0:T(8,128)(2,1)S(1)}, u32[]{:S(2)}, u32[]{:S(2)}) async-start(bf16[64,32,512]{2,1,0:T(8,128)(2,1)} %shard_map.124), calls=%async_computation.2 | async-start | bytes 4194304 | tf_op jit(solution)/shard_map/all_to_all | solution.py:400
  242.4 0.0 copy-done.2
  242.4 0.8 copy.24.key_bias
  243.2 29.7 %shard_map.125 = bf16[2048,256]{1,0:T(8,128)(2,1)} custom-call(f32[256,1]{1,0:T(8,128)} %copy.24.key_bias, bf16[2,256,256]{2,1,0:T(8,128)(2,1)} %score_proj.1, bf16[2,256,256]{2,1,0:T(8,128)(2,1)} %value_gate.1, bf16[256,256]{1,0:T(8,128)(2,1)} %column_out.1, bf16[64,64,256]{2,1,0:T(8,128)(2,1)} %all_to_all.20.products.got), custom_call_target="tpu_custom_call" | custom-call | flops 1879048192 | bytes 2097152 | tf_op jit(solution)/shard_map/pallas_call | solution.py:371
  272.9 65.1 %all-to-all-done.2 = bf16[64,32,512]{2,1,0:T(8,128)(2,1)S(1)} async-done(((bf16[64,32,512]{2,1,0:T(8,128)(2,1)}), bf16[64,32,512]{2,1,0:T(8,128)(2,1)S(1)}, u32[]{:S(2)}, u32[]{:S(2)}) %all-to-all-start.2) | async-done | bytes 2097184 | tf_op jit(solution)/shard_map/all_to_all | solution.py:400
  338.0 0.2 slice_bitcast_fusion
  338.2 0.8 fusion
  339.0 1.1 copy.47
  340.1 8.6 %all-to-all-start.3 = ((bf16[64,16,512]{2,1,0:T(8,128)(2,1)}), bf16[64,16,512]{2,1,0:T(8,128)(2,1)S(1)}, u32[]{:S(2)}, u32[]{:S(2)}) async-start(bf16[64,16,512]{2,1,0:T(8,128)(2,1)} %bitcast.52), calls=%async_computation.3 | async-start | bytes 2097152 | tf_op jit(solution)/shard_map/all_to_all | solution.py:400
  348.7 6.5 %shard_map.126 = (f32[8,128,512]{2,1,0:T(8,128)}, bf16[8,128,512]{2,1,0:T(8,128)(2,1)}) custom-call(s32[1]{0:T(128)} %bitcast.first, s32[512]{0:T(512)} %chain_each.7, s32[1,512]{1,0:T(1,128)} %bitcast.59, f32[2,128]{1,0:T(2,128)} %embed.7, bf16[2,128,128]{2,1,0:T(8,128)(2,1)} %weights_out.5, bf16[2,128,640]{2,1,0:T(8,128)(2,1)} %weights_in.7, ...), custom_call_target="tpu_custom_call" | custom-call | tf_op jit(solution)/shard_map/pallas_call | solution.py:335
  355.3 44.9 %all-to-all-done.3.products = bf16[64,16,512]{2,1,0:T(8,128)(2,1)S(1)} async-done(((bf16[64,16,512]{2,1,0:T(8,128)(2,1)}), bf16[64,16,512]{2,1,0:T(8,128)(2,1)S(1)}, u32[]{:S(2)}, u32[]{:S(2)}) %all-to-all-start.3) | async-done | bytes 1048608 | tf_op jit(solution)/shard_map/all_to_all | solution.py:400
  400.2 0.0 copy-start.1
  400.2 1.0 copy-done.1
  401.2 4.6 %shard_map.127 = bf16[8,512,128]{2,1,0:T(8,128)(2,1)} custom-call(bf16[2,128,128]{2,1,0:T(8,128)(2,1)} %weights_out.5, bf16[64,16,512]{2,1,0:T(8,128)(2,1)} %copy-done.1, f32[8,128,512]{2,1,0:T(8,128)} %get-tuple-element.26.pair_from, bf16[8,128,512]{2,1,0:T(8,128)(2,1)} %get-tuple-element.27.gate_from), custom_call_target="tpu_custom_call" | custom-call | tf_op jit(solution)/shard_map/pallas_call | solution.py:350
  (1 shorter events, 0.0 us)
Async XLA Ops:
  0.6 27.2 %copy-start = (bf16[4,512,256]{2,1,0:T(8,128)(2,1)S(1)}, bf16[4,512,256]{2,1,0:T(8,128)(2,1)}, u32[]{:S(2)}) copy-start(bf16[4,512,256]{2,1,0:T(8,128)(2,1)} %param.11) | copy-start | bytes 3145732
  6.2 112.9 %all-to-all-start = ((bf16[64,32,512]{2,1,0:T(8,128)(2,1)}), bf16[64,32,512]{2,1,0:T(8,128)(2,1)}, u32[]{:S(2)}, u32[]{:S(2)}) async-start(bf16[64,32,512]{2,1,0:T(8,128)(2,1)} %shard_map.122), calls=%async_computation | async-start | bytes 4194304 | tf_op jit(solution)/shard_map/all_to_all | solution.py:400
  233.8 8.7 %copy-start.2 = (s32[256]{0:T(256)S(1)}, s32[256]{0:T(256)}, u32[]{:S(2)}) copy-start(s32[256]{0:T(256)} %param.14) | copy-start | bytes 3076
  233.8 104.2 %all-to-all-start.2 = ((bf16[64,32,512]{2,1,0:T(8,128)(2,1)}), bf16[64,32,512]{2,1,0:T(8,128)(2,1)S(1)}, u32[]{:S(2)}, u32[]{:S(2)}) async-start(bf16[64,32,512]{2,1,0:T(8,128)(2,1)} %shard_map.124), calls=%async_computation.2 | async-start | bytes 4194304 | tf_op jit(solution)/shard_map/all_to_all | solution.py:400
  340.1 60.1 %all-to-all-start.3 = ((bf16[64,16,512]{2,1,0:T(8,128)(2,1)}), bf16[64,16,512]{2,1,0:T(8,128)(2,1)S(1)}, u32[]{:S(2)}, u32[]{:S(2)}) async-start(bf16[64,16,512]{2,1,0:T(8,128)(2,1)} %bitcast.52), calls=%async_computation.3 | async-start | bytes 2097152 | tf_op jit(solution)/shard_map/all_to_all | solution.py:400
  400.2 1.0 copy-start.1

commit v5 on v3

--- a/solution.py
+++ b/solution.py
@@ -139,6 +139,7 @@
     pair_sum,
     gate,
     pair_next,
+    updates,
     sems,
     next_sems,
 ):
@@ -150,19 +151,21 @@
     widen(products, wide)
     weights, turned = turn(weights_in[1][:, : 4 * width]), turn(weights_out[0])
     crop = crop_all[...].astype(jnp.float32)
-    leaving = []
+    for row in range(rows):
+        updates[row] = update_row(row, rows, wide, turned)
+    for copies in arriving:
+        for copy in copies:
+            copy.wait()
     for row in range(rows):
         mask = crop * crop_each[first[0] + row].astype(jnp.float32)
-        update = update_row(row, rows, wide, turned)
-        for copy in arriving[row]:
+        channels = pair_sum[row] + gate[row] * updates[row]
+        pair_next[row] = channels
+        stage_row(row, rows, channels, weights, mask, staged)
+    leaving = [start_copies((pair_next,), (pair_far,), next_sems, row) for row in range(rows)]
+    collect(staged, parts)
+    for copies in leaving:
+        for copy in copies:
             copy.wait()
-        channels = pair_sum[row] + gate[row] * update
-        pair_next[row] = channels
-        leaving += start_copies((pair_next,), (pair_far,), next_sems, row)
-        stage_row(row, rows, channels, weights, mask, staged)
-    collect(staged, parts)
-    for copy in leaving:
-        copy.wait()
 
 
 def middle_gate_kernel(weights_in, pair_sum, gate):
@@ -172,7 +175,7 @@
 
 
 def close_kernel(
-    weights_out, products, pair_from, gate_from, pair_new, wide, pair_sum, gate, sems
+    weights_out, products, pair_from, gate_from, pair_new, wide, pair_sum, gate, updates, sems
 ):
     rows = pair_sum.shape[0]
     arriving = [
@@ -181,10 +184,13 @@
     widen(products, wide)
     turned = turn(weights_out[1])
     for row in range(rows):
-        update = update_row(row, rows, wide, turned)
-        for copy in arriving[row]:
+        updates[row] = update_row(row, rows, wide, turned)
+    for copies in arriving:
+        for copy in copies:
             copy.wait()
-        pair_new[row] = (pair_sum[row] + gate[row] * update).T.astype(pair_new.dtype)
+    for row in range(rows):
+        channels = pair_sum[row] + gate[row] * updates[row]
+        pair_new[row] = channels.T.astype(pair_new.dtype)
 
 
 def attend_kernel(key_bias, score_proj, value_gate, column_out, got, out, wide, staged):
@@ -284,7 +290,7 @@
         + [pl.BlockSpec((devices, held // 2, lanes), lambda step: (0, 0, 0)), FAR, FAR],
         out_specs=(HERE, FAR),
         out_shape=(parts, pair_next),
-        scratch_shapes=[wide, staged, near, near, near]
+        scratch_shapes=[wide, staged, near, near, near, near]
         + [pltpu.SemaphoreType.DMA((2, rows)), pltpu.SemaphoreType.DMA((1, rows))],
         compiler_params=KERNEL,
     )(first, crop, crop[None], weights_out, weights_in, products, pair_sum, gate)
@@ -309,7 +315,7 @@
         in_specs=[HERE] * 2 + [FAR] * 2,
         out_specs=HERE,
         out_shape=jax.ShapeDtypeStruct((rows, side, channels), jnp.bfloat16),
-        scratch_shapes=[wide, near, near, pltpu.SemaphoreType.DMA((2, rows))],
+        scratch_shapes=[wide, near, near, near, pltpu.SemaphoreType.DMA((2, rows))],
         compiler_params=KERNEL,
     )(weights_out, products, pair_sum, gate)
 

time: 408 us -> 407 us (level)
  no operation moved by 1% of the time
where the time goes in v5:
time: 407 us
  waiting for transfers between devices  202 us (50%)
  blocking collectives  104 us (26%)
  Pallas kernels  57.2 us (14%)
  starting transfers between devices  34.5 us (8%)
  local copies, waits for them, and re-layouts  6.64 us (2%)
    all_to_all x3, waiting for transfers between devices, exchange_blocks(): lax.all_to_all(blocks, 'dap', split_axis=0, concat_axis=0, tiled=True)  202 us
    all_to_all x1, blocking collectives, exchange_blocks(): lax.all_to_all(blocks, 'dap', split_axis=0, concat_axis=0, tiled=True)  104 us
    all_to_all x3, starting transfers between devices, exchange_blocks(): lax.all_to_all(blocks, 'dap', split_axis=0, concat_axis=0, tiled=True)  34.5 us
    pallas_call x1, Pallas kernels, attend_columns(): pl.pallas_call(attend_kernel, grid=(1,), in_specs=[HERE] * 4 + [pl.BlockS...  29.7 us
    pallas_call x1, Pallas kernels, middle_pair(): pl.pallas_call(middle_kernel, grid=(1,), in_specs=[EACH] * 2 + [HERE] * 3...  8.25 us
  transfers between devices with their start and end apart: 3, of which 3 were waited for; matrix products, arithmetic and copies ran while one was open for 1% of the time, Pallas kernels for 9%

profile of v5, /device:TPU:1, one launch (start us, length us, event | category | flops | bytes accessed | tf_op | source)
XLA Modules:
  0.0 406.5 jit_solution(8566118698846830094)
XLA Ops:
  0.6 0.0 copy-start
  0.6 5.6 %shard_map.122 = bf16[64,32,512]{2,1,0:T(8,128)(2,1)} custom-call(s32[1]{0:T(128)} %bitcast.first, s32[512]{0:T(512)} %crop_each.3, s32[512]{0:T(512)} %chain_each.3, s32[1,512]{1,0:T(1,128)} %bitcast.59, s32[1,512]{1,0:T(1,128)} %bitcast.57, f32[2,128]{1,0:T(2,128)} %embed.3, bf16[2,128,640]{2,1,0:T(8,128)(2,1)} %weights_in.7, bf16[8,512,128]{2,1,0:T(8,128)(2,1)} %pair_act.3), custom_call_target="tpu_custom_call" | custom-call | tf_op jit(solution)/shard_map/pallas_call | solution.py:259
  6.3 17.2 %all-to-all-start = ((bf16[64,32,512]{2,1,0:T(8,128)(2,1)}), bf16[64,32,512]{2,1,0:T(8,128)(2,1)S(1)}, u32[]{:S(2)}, u32[]{:S(2)}) async-start(bf16[64,32,512]{2,1,0:T(8,128)(2,1)} %shard_map.122), calls=%async_computation | async-start | bytes 4194304 | tf_op jit(solution)/shard_map/all_to_all | solution.py:357
  23.5 4.8 %shard_map.123 = (f32[8,128,512]{2,1,0:T(8,128)}, f32[8,128,512]{2,1,0:T(8,128)}) custom-call(s32[1]{0:T(128)} %bitcast.first, s32[512]{0:T(512)} %chain_each.3, s32[1,512]{1,0:T(1,128)} %bitcast.58, f32[2,128]{1,0:T(2,128)} %embed.3, bf16[2,128,640]{2,1,0:T(8,128)(2,1)} %weights_in.7, bf16[8,512,128]{2,1,0:T(8,128)(2,1)} %pair_act.3), custom_call_target="tpu_custom_call" | custom-call | tf_op jit(solution)/shard_map/pallas_call | solution.py:271
  28.3 0.0 copy-done
  28.3 0.1 copy_bitcast_fusion.3
  28.5 1.6 concatenate.3
  30.1 89.0 %all-to-all-done = bf16[64,32,512]{2,1,0:T(8,128)(2,1)S(1)} async-done(((bf16[64,32,512]{2,1,0:T(8,128)(2,1)}), bf16[64,32,512]{2,1,0:T(8,128)(2,1)S(1)}, u32[]{:S(2)}, u32[]{:S(2)}) %all-to-all-start) | async-done | bytes 2097184 | tf_op jit(solution)/shard_map/all_to_all | solution.py:357
  119.1 0.2 slice_bitcast_fusion.2
  119.3 0.7 convolution_convert_fusion.1
  120.0 0.0 copy-start.1
  120.0 0.1 copy.23
  120.2 1.4 copy-done.1
  121.6 0.1 constant_dynamic-update-slice_fusion
  121.7 104.1 %all_to_all.20.products.got = bf16[64,64,256]{2,1,0:T(8,128)(2,1)} all-to-all(bf16[64,64,256]{2,1,0:T(8,128)(2,1)S(1)} %constant_dynamic-update-slice_fusion), channel_id=1, replica_groups=mesh['dp'=8,'dap'=64] {'dap'}, dimensions={0} | all-to-all | bytes 4194304 | tf_op jit(solution)/shard_map/all_to_all | solution.py:357
  225.8 8.2 %shard_map.124 = (bf16[64,32,512]{2,1,0:T(8,128)(2,1)}, f32[8,128,512]{2,1,0:T(8,128)}) custom-call(s32[1]{0:T(128)} %bitcast.first, s32[512]{0:T(512)} %crop_each.3, s32[1,512]{1,0:T(1,128)} %bitcast.60, bf16[2,128,128]{2,1,0:T(8,128)(2,1)} %weights_out.3, bf16[2,128,640]{2,1,0:T(8,128)(2,1)} %weights_in.7, bf16[64,64,256]{2,1,0:T(8,128)(2,1)} %all_to_all.20.products.got, ...), custom_call_target="tpu_custom_call" | custom-call | tf_op jit(solution)/shard_map/pallas_call | solution.py:285
  234.1 0.0 copy-start.3
  234.1 8.7 %all-to-all-start.2 = ((bf16[64,32,512]{2,1,0:T(8,128)(2,1)}), bf16[64,32,512]{2,1,0:T(8,128)(2,1)S(1)}, u32[]{:S(2)}, u32[]{:S(2)}) async-start(bf16[64,32,512]{2,1,0:T(8,128)(2,1)} %get-tuple-element.24), calls=%async_computation.2 | async-start | bytes 4194304 | tf_op jit(solution)/shard_map/all_to_all | solution.py:357
  242.8 0.0 copy-done.3
  242.8 0.8 copy.24.key_bias
  243.6 29.7 %shard_map.125 = bf16[2048,256]{1,0:T(8,128)(2,1)} custom-call(f32[256,1]{1,0:T(8,128)} %copy.24.key_bias, bf16[2,256,256]{2,1,0:T(8,128)(2,1)} %score_proj.1, bf16[2,256,256]{2,1,0:T(8,128)(2,1)} %value_gate.1, bf16[256,256]{1,0:T(8,128)(2,1)} %column_out.1, bf16[64,64,256]{2,1,0:T(8,128)(2,1)} %all_to_all.20.products.got), custom_call_target="tpu_custom_call" | custom-call | flops 1879048192 | bytes 2097152 | tf_op jit(solution)/shard_map/pallas_call | solution.py:328
  273.2 65.1 %all-to-all-done.2 = bf16[64,32,512]{2,1,0:T(8,128)(2,1)S(1)} async-done(((bf16[64,32,512]{2,1,0:T(8,128)(2,1)}), bf16[64,32,512]{2,1,0:T(8,128)(2,1)S(1)}, u32[]{:S(2)}, u32[]{:S(2)}) %all-to-all-start.2) | async-done | bytes 2097184 | tf_op jit(solution)/shard_map/all_to_all | solution.py:357
  338.3 0.2 slice_bitcast_fusion
  338.5 0.8 fusion
  339.3 1.1 copy.47
  340.4 8.6 %all-to-all-start.3 = ((bf16[64,16,512]{2,1,0:T(8,128)(2,1)}), bf16[64,16,512]{2,1,0:T(8,128)(2,1)S(1)}, u32[]{:S(2)}, u32[]{:S(2)}) async-start(bf16[64,16,512]{2,1,0:T(8,128)(2,1)} %bitcast.52), calls=%async_computation.3 | async-start | bytes 2097152 | tf_op jit(solution)/shard_map/all_to_all | solution.py:357
  349.0 3.9 shard_map.126.gate_from
  352.9 47.6 %all-to-all-done.3.products = bf16[64,16,512]{2,1,0:T(8,128)(2,1)S(1)} async-done(((bf16[64,16,512]{2,1,0:T(8,128)(2,1)}), bf16[64,16,512]{2,1,0:T(8,128)(2,1)S(1)}, u32[]{:S(2)}, u32[]{:S(2)}) %all-to-all-start.3) | async-done | bytes 1048608 | tf_op jit(solution)/shard_map/all_to_all | solution.py:357
  400.5 0.0 copy-start.2
  400.5 1.0 copy-done.2
  401.5 4.9 %shard_map.127 = bf16[8,512,128]{2,1,0:T(8,128)(2,1)} custom-call(bf16[2,128,128]{2,1,0:T(8,128)(2,1)} %weights_out.3, bf16[64,16,512]{2,1,0:T(8,128)(2,1)} %copy-done.2, f32[8,128,512]{2,1,0:T(8,128)} %get-tuple-element.29.pair_sum.pair_from, f32[8,128,512]{2,1,0:T(8,128)} %shard_map.126.gate_from), custom_call_target="tpu_custom_call" | custom-call | tf_op jit(solution)/shard_map/pallas_call | solution.py:313
  (1 shorter events, 0.0 us)
Async XLA Ops:
  0.6 27.7 %copy-start = (bf16[4,512,256]{2,1,0:T(8,128)(2,1)S(1)}, bf16[4,512,256]{2,1,0:T(8,128)(2,1)}, u32[]{:S(2)}) copy-start(bf16[4,512,256]{2,1,0:T(8,128)(2,1)} %param.11) | copy-start | bytes 3145732
  6.3 112.8 %all-to-all-start = ((bf16[64,32,512]{2,1,0:T(8,128)(2,1)}), bf16[64,32,512]{2,1,0:T(8,128)(2,1)S(1)}, u32[]{:S(2)}, u32[]{:S(2)}) async-start(bf16[64,32,512]{2,1,0:T(8,128)(2,1)} %shard_map.122), calls=%async_computation | async-start | bytes 4194304 | tf_op jit(solution)/shard_map/all_to_all | solution.py:357
  120.0 1.6 copy-start.1
  234.1 8.7 %copy-start.3 = (s32[256]{0:T(256)S(1)}, s32[256]{0:T(256)}, u32[]{:S(2)}) copy-start(s32[256]{0:T(256)} %param.14) | copy-start | bytes 3076
  234.1 104.2 %all-to-all-start.2 = ((bf16[64,32,512]{2,1,0:T(8,128)(2,1)}), bf16[64,32,512]{2,1,0:T(8,128)(2,1)S(1)}, u32[]{:S(2)}, u32[]{:S(2)}) async-start(bf16[64,32,512]{2,1,0:T(8,128)(2,1)} %get-tuple-element.24), calls=%async_computation.2 | async-start | bytes 4194304 | tf_op jit(solution)/shard_map/all_to_all | solution.py:357
  340.4 60.1 %all-to-all-start.3 = ((bf16[64,16,512]{2,1,0:T(8,128)(2,1)}), bf16[64,16,512]{2,1,0:T(8,128)(2,1)S(1)}, u32[]{:S(2)}, u32[]{:S(2)}) async-start(bf16[64,16,512]{2,1,0:T(8,128)(2,1)} %bitcast.52), calls=%async_computation.3 | async-start | bytes 2097152 | tf_op jit(solution)/shard_map/all_to_all | solution.py:357
  400.5 1.0 copy-start.2
